TPU v7x, 128 devices: a whole 4x4x4 slice. The times are simulated.
128 devices in a mesh: slide: 16 (over y, x), seq: 8 (over z, core).
Axes of the slice: x: 4, y: 4, z: 4, core: 2. Of those that a mesh axis runs over, the one named last changes fastest.
Arguments:
- tile_feats: bfloat16 [49152, 1536], P(('slide', 'seq')), may hold values from -6 to 6
- norm_gain: float32 [1536], replicated, may hold values from 0.1 to 1.9
- w_embed: bfloat16 [1536, 768], replicated, may hold values from -0.15625 to 0.15625
- slide_of_tile: int32 [49152, 1], P(('slide', 'seq')), may hold values from 0 to 15; in each aligned block of 384 rows (0 to 383, 384 to 767, ...) at most 48 rows name the same one
- w_qkv: bfloat16 [768, 2304], replicated, may hold values from -2 to 2
- w_out: bfloat16 [768, 768], replicated, may hold values from -0.21875 to 0.21875
- cotangent: bfloat16 [16, 6144, 768], P('slide', 'seq'), may hold values from -6 to 6
Outputs:
- attended: bfloat16 [16, 6144, 768], P('slide', 'seq')
- grad_qkv: float32 [768, 2304], P(('slide', 'seq'))
- grad_out: float32 [768, 768], P(('slide', 'seq'))
Inputs may be any that keep to these rules, and one draw needn't show every extreme that they name: `slide_of_tile`: among one device's 384 tiles at most 48 name the same slide, a bound that some block reaches of them.
All inputs are finite; a program needn't handle non-finite values.
Results may differ from a plain program's by a relative error of at most 0.03.
The roundings to bfloat16 on the way count: a program that leaves them out, or rounds other values in their place, can miss the bound.
Values may be sent and summed in bfloat16 or wider, within the bound.
A program may use at most 128 MiB of HBM per device.

v0:
```python
import jax
import jax.numpy as jnp
from jax import lax
from jax.sharding import PartitionSpec as P

HEADS = 12
CAP = 48
RATE = 8


masked_value = -1e30


def embed_tiles(feats, norm_gain, w_embed):
    values = feats.astype(jnp.float32)
    center = jnp.mean(values, axis=-1, keepdims=True)
    spread = jnp.mean((values - center) ** 2, axis=-1, keepdims=True)
    normed = ((values - center) * lax.rsqrt(spread + 1e-06) * norm_gain).astype(jnp.bfloat16)
    return jnp.dot(normed, w_embed, preferred_element_type=jnp.float32).astype(jnp.bfloat16)


def place_tiles(embedded, targets, slides):
    one_hot = (targets[:, None] == jnp.arange(slides, dtype=jnp.int32)[None, :]).astype(jnp.int32)
    order_rank = jnp.sum((jnp.cumsum(one_hot, axis=0) - 1) * one_hot, axis=1)
    slot_index = targets * CAP + order_rank
    placing = (jnp.arange(slides * CAP, dtype=jnp.int32)[:, None] == slot_index[None, :]).astype(
        jnp.bfloat16
    )
    buffer = jnp.dot(placing, embedded, preferred_element_type=jnp.float32).astype(jnp.bfloat16)
    return (buffer, jnp.sum(one_hot, axis=0))


def head_pass(query, local_keys, local_values, far_keys, far_values, d_head, key_mask):
    scale = query.shape[-1] ** (-0.5)
    keys_all = jnp.concatenate([local_keys, far_keys], axis=0)
    values_all = jnp.concatenate([local_values, far_values], axis=0)
    scores = jnp.dot(query, keys_all.T, preferred_element_type=jnp.float32) * scale
    scores = jnp.where(key_mask[None, :], scores, masked_value)
    peak = jnp.max(scores, axis=-1, keepdims=True)
    raw_weights = jnp.exp(scores - peak)
    prob_exact = raw_weights / jnp.sum(raw_weights, axis=-1, keepdims=True)
    prob_bf16 = prob_exact.astype(jnp.bfloat16)
    head_output = jnp.dot(prob_bf16, values_all, preferred_element_type=jnp.float32).astype(
        jnp.bfloat16
    )
    grad_p = jnp.dot(d_head, values_all.T, preferred_element_type=jnp.float32)
    row_delta = jnp.sum(
        d_head.astype(jnp.float32) * head_output.astype(jnp.float32), axis=-1, keepdims=True
    )
    grad_s = (prob_exact * (grad_p - row_delta)).astype(jnp.bfloat16)
    grad_query = (jnp.dot(grad_s, keys_all, preferred_element_type=jnp.float32) * scale).astype(
        jnp.bfloat16
    )
    grad_key = jnp.dot(grad_s.T, query, preferred_element_type=jnp.float32) * scale
    grad_value = jnp.dot(prob_bf16.T, d_head, preferred_element_type=jnp.float32)
    local_count = local_keys.shape[0]
    return (
        head_output,
        grad_query,
        grad_key[:local_count].astype(jnp.bfloat16),
        grad_value[:local_count].astype(jnp.bfloat16),
        grad_key[local_count:],
        grad_value[local_count:],
    )


def block_pass(rows_in, valid, qkv, kv_dilated, valid_dilated, grad_rows, w_out):
    width = rows_in.shape[1]
    head_size = width // HEADS

    def to_heads(array):
        return array.reshape(array.shape[0], HEADS, head_size).transpose(1, 0, 2)

    def from_heads(array):
        return array.transpose(1, 0, 2).reshape(array.shape[1], HEADS * head_size)

    masked_grad = (grad_rows.astype(jnp.float32) * valid[:, None]).astype(jnp.bfloat16)
    d_heads = jnp.dot(masked_grad, w_out.T, preferred_element_type=jnp.float32).astype(jnp.bfloat16)
    key_mask = jnp.concatenate([valid, valid_dilated]) > 0.5
    results = lax.map(
        lambda group: head_pass(*group, key_mask),
        (
            to_heads(qkv[:, :width]),
            to_heads(qkv[:, width : 2 * width]),
            to_heads(qkv[:, 2 * width :]),
            to_heads(kv_dilated[:, :width]),
            to_heads(kv_dilated[:, width:]),
            to_heads(d_heads),
        ),
    )
    heads_out = from_heads(results[0])
    mixed = rows_in.astype(jnp.float32) + jnp.dot(
        heads_out, w_out, preferred_element_type=jnp.float32
    )
    output = (mixed * valid[:, None]).astype(jnp.bfloat16)
    grad_mix = jnp.dot(heads_out.T, masked_grad, preferred_element_type=jnp.float32)
    local_grads = jnp.concatenate(
        [from_heads(results[1]), from_heads(results[2]), from_heads(results[3])], axis=1
    )
    grad_proj = jnp.dot(rows_in.T, local_grads, preferred_element_type=jnp.float32)
    dilated_grad = jnp.concatenate([from_heads(results[4]), from_heads(results[5])], axis=1)
    return (output, grad_proj, grad_mix, dilated_grad)


def split_product(rows_dilated, grad_full):
    high_part = lax.optimization_barrier(grad_full.astype(jnp.bfloat16))
    low_part = (grad_full - high_part.astype(jnp.float32)).astype(jnp.bfloat16)
    contract = (((0,), (0,)), ((), ()))
    upper = lax.dot_general(rows_dilated, high_part, contract, preferred_element_type=jnp.float32)
    lower = lax.dot_general(rows_dilated, low_part, contract, preferred_element_type=jnp.float32)
    return upper + lower


def shards(tile_feats, norm_gain, w_embed, slide_of_tile, w_qkv, w_out, cotangent):
    width = w_out.shape[0]
    slides = lax.axis_size("slide")
    blocks = lax.axis_size("seq")
    embedded = embed_tiles(tile_feats, norm_gain, w_embed)
    buffer, counts = place_tiles(embedded, slide_of_tile[:, 0], slides)
    received, arrived = (
        lax.all_to_all(
            buffer.reshape(slides, CAP, width), "slide", split_axis=0, concat_axis=0, tiled=True
        ),
        lax.all_to_all(counts.reshape(slides, 1), "slide", split_axis=0, concat_axis=0, tiled=True),
    )
    rows_in = received.reshape(slides * CAP, width)
    valid = (
        (jnp.arange(CAP, dtype=jnp.int32)[None, :] < arrived)
        .astype(jnp.float32)
        .reshape(slides * CAP)
    )
    qkv = jnp.dot(rows_in, w_qkv, preferred_element_type=jnp.float32).astype(jnp.bfloat16)
    rows_dilated = rows_in[::RATE]
    valid_dilated = valid[::RATE].astype(jnp.bfloat16)
    kv_dilated, valid_far = (
        lax.all_gather(qkv[::RATE, width:], "seq", axis=0, tiled=True),
        lax.all_gather(valid_dilated, "seq", axis=0, tiled=True),
    )
    output, grad_proj, grad_mix, dilated_grad = block_pass(
        rows_in, valid, qkv, kv_dilated, valid_far.astype(jnp.float32), cotangent[0], w_out
    )
    owned_grad = lax.psum_scatter(dilated_grad, "seq", scatter_dimension=0, tiled=True)
    dilated_term = split_product(rows_dilated, owned_grad)
    grad_proj = jnp.concatenate([grad_proj[:, :width], grad_proj[:, width:] + dilated_term], axis=1)
    factor = (slides * blocks * rows_in.shape[0]) ** (-0.5)
    grad_qkv, grad_out = (
        lax.psum_scatter(grad_proj * factor, ("slide", "seq"), scatter_dimension=0, tiled=True),
        lax.psum_scatter(grad_mix * factor, ("slide", "seq"), scatter_dimension=0, tiled=True),
    )
    return (output[None], grad_qkv, grad_out)


def solution(mesh):
    return jax.shard_map(
        shards,
        mesh=mesh,
        in_specs=(
            P(("slide", "seq"), None),
            P(),
            P(),
            P(("slide", "seq"), None),
            P(),
            P(),
            P("slide", "seq", None),
        ),
        out_specs=(P("slide", "seq", None), P(("slide", "seq"), None), P(("slide", "seq"), None)),
        check_vma=False,
    )
```

profile of v0, /device:TPU:1, one launch (start us, length us, event | category | flops | bytes accessed | tf_op | source)
XLA Modules:
  0.0 1077.6 jit_solution(17120862363019863599)
XLA Ops:
  16.4 4.9 convolution_convert_fusion.1
  21.3 25.0 %all_to_all.14 = bf16[16,48,768]{2,1,0:T(8,128)(2,1)S(1)} all-to-all(bf16[16,48,768]{2,1,0:T(8,128)(2,1)} %bitcast.168), channel_id=1, replica_groups=mesh['slide'=16,'seq'=8] {'slide'}, dimensions={0} | all-to-all | bytes 2359296 | tf_op jit(solution)/shard_map/all_to_all | solution.py:121
  47.4 4.3 convolution_convert_fusion
  51.7 3.7 slice.56
  56.1 3.5 all-to-all-start.1
  60.9 4.9 all-to-all-done.1
  66.8 16.5 %all-reduce = bf16[768]{0:T(1024)(128)(2,1)S(1)} all-reduce(bf16[768]{0:T(1024)(128)(2,1)S(1)} %dynamic-update-slice), channel_id=1, replica_groups=mesh['slide'=16,'seq'=8] {'seq'}, use_global_device_ids=true, to_apply=%add | all-reduce | flops 768 | bytes 3072
  83.4 4.0 convolution_convert_fusion.2
  96.7 276.5 %while.20 = (s32[]{:T(128)}, bf16[12,768,64]{1,2,0:T(8,128)(2,1)}, bf16[12,768,64]{1,2,0:T(8,128)(2,1)}, bf16[12,768,64]{1,2,0:T(8,128)(2,1)}, bf16[12,768,64]{1...) while((s32[]{:T(128)}, bf16[12,768,64]{1,2,0:T(8,128)(2,1)}, ...), condition=%wide.region_10.11_spmd, body=%wide.region_6.0_spmd.sunk | while | flops 926856960 | bytes 64222908 | solution.py:80
  101.7 3.2 fusion.108
  107.0 4.0 bitcast_dynamic-update-slice_fusion.2
  124.8 3.2 fusion.108
  130.1 4.0 bitcast_dynamic-update-slice_fusion.2
  147.8 3.2 fusion.108
  153.1 4.0 bitcast_dynamic-update-slice_fusion.2
  170.8 3.2 fusion.108
  176.1 4.0 bitcast_dynamic-update-slice_fusion.2
  193.8 3.2 fusion.108
  199.2 4.0 bitcast_dynamic-update-slice_fusion.2
  216.9 3.2 fusion.108
  222.2 4.0 bitcast_dynamic-update-slice_fusion.2
  239.9 3.2 fusion.108
  245.3 4.0 bitcast_dynamic-update-slice_fusion.2
  263.0 3.2 fusion.108
  268.3 4.0 bitcast_dynamic-update-slice_fusion.2
  286.0 3.2 fusion.108
  291.3 4.0 bitcast_dynamic-update-slice_fusion.2
  309.1 3.2 fusion.108
  314.4 4.0 bitcast_dynamic-update-slice_fusion.2
  332.1 3.2 fusion.108
  337.4 4.0 bitcast_dynamic-update-slice_fusion.2
  355.1 3.2 fusion.108
  360.4 4.0 bitcast_dynamic-update-slice_fusion.2
  373.2 4.8 pad_maximum_fusion.6
  378.0 6.1 copy.50
  386.4 4.6 fusion.38
  395.2 3.9 convolution_multiply_fusion.2
  399.1 17.2 %reduce-scatter.8.cloned.1.call-done = f32[96,1536]{1,0:T(8,128)} async-done(((f32[768,1536]{1,0:T(8,128)}), f32[96,1536]{1,0:T(8,128)}) %reduce-scatter.8.cloned.1.call-update) | async-done | bytes 589840
  418.5 3.4 slice_add_fusion
  421.8 3.6 maximum_multiply_fusion
  425.4 361.7 %fusion.70 = (f32[8,2304]{1,0:T(8,128)}, f32[8,768]{1,0:T(8,128)S(1)}) fusion(f32[768,2304]{1,0:T(8,128)} %maximum_multiply_fusion, f32[768,768]{1,0:T(8,128)} %convolution_multiply_fusion.2), kind=kCustom, calls=%all-reduce-scatter.2 | all-reduce-scatter fusion | flops 3145729 | bytes 9535488
  801.8 14.6 %collective-permute-start.41 = (f32[8,768]{1,0:T(8,128)S(1)}, f32[8,768]{1,0:T(8,128)S(1)}, u32[]{:S(2)}, u32[]{:S(2)}) collective-permute-start(f32[8,768]{1,0:T(8,128)S(1)} %get-tuple-element.161), channel_id=1, source_target_pairs={{0,10},{1,11},{2,12},{3,13},{4,14},{5,15},{6,16},{7,17},{8,18},{9,... | collective-permute-start | bytes 73736
  820.7 4.9 collective-permute-start.44
  825.6 13.5 %collective-permute-start.45 = (f32[8,768]{1,0:T(8,128)S(1)}, f32[8,768]{1,0:T(8,128)S(1)}, u32[]{:S(2)}, u32[]{:S(2)}) collective-permute-start(f32[8,768]{1,0:T(8,128)S(1)} %get-tuple-element.161), channel_id=1, source_target_pairs={{0,14},{1,15},{2,16},{3,17},{4,18},{5,19},{6,20},{7,21},{8,22},{9,... | collective-permute-start | bytes 73736
  839.1 3.8 collective-permute-start.46
  842.9 4.6 collective-permute-start.47
  851.1 3.4 collective-permute-start.50
  876.1 3.3 collective-permute-start.60
  879.5 3.5 collective-permute-start.61
  886.1 3.3 collective-permute-start.10
  889.4 3.9 collective-permute-start.11
  893.4 4.6 collective-permute-start.12
  898.0 3.4 collective-permute-start.13
  901.5 3.4 collective-permute-start.14
  906.6 4.3 collective-permute-start.16
  915.0 2.9 collective-permute-start.19
  920.7 3.4 collective-permute-start.20
  933.3 4.6 collective-permute-start.27
  946.1 3.5 collective-permute-start.4
  949.7 3.8 fusion.52
  953.6 46.2 %concatenate.23 = f32[262,768]{1,0:T(8,128)} concatenate(f32[6,768]{1,0:T(8,128)S(1)} %collective-permute-done.63, f32[8,768]{1,0:T(8,128)} %collective-permute-done.62, f32[8,768]{1,0:T(8,128)} %collective-permute-done.61, f32[8,768]{1,0:T(8,128)} %collective-permute-done.60, f32[8,768]{1,0:T(8,128)S(1)} %collective-permute-done.59, f32[8,768]{1,0:T(8,128)S(1)} %collective-permute-done.58, ...), dimensions={0} | concatenate | bytes 1609728
  1004.5 3.3 collective-permute-start.7
  1009.7 3.8 collective-permute-start.9
  1015.1 54.1 %concatenate.22 = f32[262,2304]{1,0:T(8,128)} concatenate(f32[6,2304]{1,0:T(8,128)} %copy-done.10, f32[8,2304]{1,0:T(8,128)} %collective-permute-done.30, f32[8,2304]{1,0:T(8,128)} %collective-permute-done.29, f32[8,2304]{1,0:T(8,128)} %collective-permute-done.28, f32[8,2304]{1,0:T(8,128)} %copy-done.30, f32[8,2304]{1,0:T(8,128)} %copy-done.29, f32[8,2304]{1,0:T(8,128)} %copy-done.28, ...), dimensions={0} | concatenate | bytes 4829184
  (452 shorter events, 302.8 us)
Async XLA Ops:
  7.2 84.8 %all-gather.2.cloned.1.call-start = ((), (), s32[]{:S(2)}) async-start(), calls=%async_computation.3 | async-start | bytes 2654208 | tf_op jit(solution)/shard_map/all_gather | solution.py:136
  56.1 9.7 all-to-all-start.1
  59.5 356.7 %reduce-scatter.8.cloned.1.call-start = ((), (), s32[]{:S(2)}) async-start(), calls=%async_computation.4 | async-start | bytes 5308416
  787.1 8.4 collective-permute-start.32
  790.3 6.5 collective-permute-start.33
  791.6 6.5 collective-permute-start.34
  792.9 6.5 collective-permute-start.35
  794.2 7.5 collective-permute-start.36
  795.6 20.9 %collective-permute-start.37 = (f32[8,768]{1,0:T(8,128)S(1)}, f32[8,768]{1,0:T(8,128)S(1)}, u32[]{:S(2)}, u32[]{:S(2)}) collective-permute-start(f32[8,768]{1,0:T(8,128)S(1)} %get-tuple-element.161), channel_id=1, source_target_pairs={{0,6},{1,7},{2,8},{3,9},{4,10},{5,11},{6,12},{7,13},{8,14},{9,15},... | collective-permute-start | bytes 73736
  796.9 22.4 %collective-permute-start.38 = (f32[8,768]{1,0:T(8,128)S(1)}, f32[8,768]{1,0:T(8,128)S(1)}, u32[]{:S(2)}, u32[]{:S(2)}) collective-permute-start(f32[8,768]{1,0:T(8,128)S(1)} %get-tuple-element.161), channel_id=1, source_target_pairs={{0,7},{1,8},{2,9},{3,10},{4,11},{5,12},{6,13},{7,14},{8,15},{9,16}... | collective-permute-start | bytes 73736
  798.2 22.5 %collective-permute-start.39 = (f32[8,768]{1,0:T(8,128)S(1)}, f32[8,768]{1,0:T(8,128)S(1)}, u32[]{:S(2)}, u32[]{:S(2)}) collective-permute-start(f32[8,768]{1,0:T(8,128)S(1)} %get-tuple-element.161), channel_id=1, source_target_pairs={{0,8},{1,9},{2,10},{3,11},{4,12},{5,13},{6,14},{7,15},{8,16},{9,17... | collective-permute-start | bytes 73736
  799.5 26.1 %collective-permute-start.40 = (f32[8,768]{1,0:T(8,128)S(1)}, f32[8,768]{1,0:T(8,128)S(1)}, u32[]{:S(2)}, u32[]{:S(2)}) collective-permute-start(f32[8,768]{1,0:T(8,128)S(1)} %get-tuple-element.161), channel_id=1, source_target_pairs={{0,9},{1,10},{2,11},{3,12},{4,13},{5,14},{6,15},{7,16},{8,17},{9,1... | collective-permute-start | bytes 73736
  801.8 37.3 %collective-permute-start.41 = (f32[8,768]{1,0:T(8,128)S(1)}, f32[8,768]{1,0:T(8,128)S(1)}, u32[]{:S(2)}, u32[]{:S(2)}) collective-permute-start(f32[8,768]{1,0:T(8,128)S(1)} %get-tuple-element.161), channel_id=1, source_target_pairs={{0,10},{1,11},{2,12},{3,13},{4,14},{5,15},{6,16},{7,17},{8,18},{9,... | collective-permute-start | bytes 73736
  816.5 26.5 %collective-permute-start.42 = (f32[8,768]{1,0:T(8,128)S(1)}, f32[8,768]{1,0:T(8,128)S(1)}, u32[]{:S(2)}, u32[]{:S(2)}) collective-permute-start(f32[8,768]{1,0:T(8,128)S(1)} %get-tuple-element.161), channel_id=1, source_target_pairs={{0,11},{1,12},{2,13},{3,14},{4,15},{5,16},{6,17},{7,18},{8,19},{9,... | collective-permute-start | bytes 73736
  819.3 28.2 %collective-permute-start.43 = (f32[8,768]{1,0:T(8,128)S(1)}, f32[8,768]{1,0:T(8,128)S(1)}, u32[]{:S(2)}, u32[]{:S(2)}) collective-permute-start(f32[8,768]{1,0:T(8,128)S(1)} %get-tuple-element.161), channel_id=1, source_target_pairs={{0,12},{1,13},{2,14},{3,15},{4,16},{5,17},{6,18},{7,19},{8,20},{9,... | collective-permute-start | bytes 73736
  820.7 28.8 %collective-permute-start.44 = (f32[8,768]{1,0:T(8,128)S(1)}, f32[8,768]{1,0:T(8,128)S(1)}, u32[]{:S(2)}, u32[]{:S(2)}) collective-permute-start(f32[8,768]{1,0:T(8,128)S(1)} %get-tuple-element.161), channel_id=1, source_target_pairs={{0,13},{1,14},{2,15},{3,16},{4,17},{5,18},{6,19},{7,20},{8,21},{9,... | collective-permute-start | bytes 73736
  825.6 25.5 %collective-permute-start.45 = (f32[8,768]{1,0:T(8,128)S(1)}, f32[8,768]{1,0:T(8,128)S(1)}, u32[]{:S(2)}, u32[]{:S(2)}) collective-permute-start(f32[8,768]{1,0:T(8,128)S(1)} %get-tuple-element.161), channel_id=1, source_target_pairs={{0,14},{1,15},{2,16},{3,17},{4,18},{5,19},{6,20},{7,21},{8,22},{9,... | collective-permute-start | bytes 73736
  839.1 15.4 %collective-permute-start.46 = (f32[8,768]{1,0:T(8,128)S(1)}, f32[8,768]{1,0:T(8,128)S(1)}, u32[]{:S(2)}, u32[]{:S(2)}) collective-permute-start(f32[8,768]{1,0:T(8,128)S(1)} %get-tuple-element.161), channel_id=1, source_target_pairs={{0,15},{1,16},{2,17},{3,18},{4,19},{5,20},{6,21},{7,22},{8,23},{9,... | collective-permute-start | bytes 73736
  842.9 14.2 %collective-permute-start.47 = (f32[8,768]{1,0:T(8,128)S(1)}, f32[8,768]{1,0:T(8,128)S(1)}, u32[]{:S(2)}, u32[]{:S(2)}) collective-permute-start(f32[8,768]{1,0:T(8,128)S(1)} %get-tuple-element.161), channel_id=1, source_target_pairs={{0,16},{1,17},{2,18},{3,19},{4,20},{5,21},{6,22},{7,23},{8,24},{9,... | collective-permute-start | bytes 73736
  847.5 10.9 %collective-permute-start.48 = (f32[8,768]{1,0:T(8,128)S(1)}, f32[8,768]{1,0:T(8,128)S(1)}, u32[]{:S(2)}, u32[]{:S(2)}) collective-permute-start(f32[8,768]{1,0:T(8,128)S(1)} %get-tuple-element.161), channel_id=1, source_target_pairs={{0,17},{1,18},{2,19},{3,20},{4,21},{5,22},{6,23},{7,24},{8,25},{9,... | collective-permute-start | bytes 73736
  849.4 10.7 collective-permute-start.49
  851.1 10.3 collective-permute-start.50
  854.5 8.5 collective-permute-start.51
  857.1 7.6 collective-permute-start.52
  858.4 9.6 collective-permute-start.53
  860.1 9.2 collective-permute-start.54
  861.4 10.3 collective-permute-start.55
  863.1 10.9 %collective-permute-start.56 = (f32[8,768]{1,0:T(8,128)S(1)}, f32[8,768]{1,0:T(8,128)S(1)}, u32[]{:S(2)}, u32[]{:S(2)}) collective-permute-start(f32[8,768]{1,0:T(8,128)S(1)} %get-tuple-element.161), channel_id=1, source_target_pairs={{0,25},{1,26},{2,27},{3,28},{4,29},{5,30},{6,31},{7,32},{8,33},{9,... | collective-permute-start | bytes 73736
  864.7 33.3 %collective-permute-start = (f32[8,2304]{1,0:T(8,128)}, f32[8,2304]{1,0:T(8,128)S(1)}, u32[]{:S(2)}, u32[]{:S(2)}) collective-permute-start(f32[8,2304]{1,0:T(8,128)} %get-tuple-element.160), channel_id=1, source_target_pairs={{0,1},{1,2},{2,3},{3,4},{4,5},{5,6},{6,7},{7,8},{8,9},{9,10},{10,1... | collective-permute-start | bytes 221192
  868.0 25.3 %collective-permute-start.31 = (f32[6,2304]{1,0:T(8,128)S(1)}, f32[6,2304]{1,0:T(8,128)S(1)}, u32[]{:S(2)}, u32[]{:S(2)}) collective-permute-start(f32[6,2304]{1,0:T(8,128)S(1)} %slice.75), channel_id=1, source_target_pairs={{0,32},{1,33},{2,34},{3,35},{4,36},{5,37},{6,38},{7,39},{8,40},{9,... | collective-permute-start | bytes 165896
  869.3 6.8 collective-permute-start.57
  871.7 7.8 collective-permute-start.58
  873.9 9.0 collective-permute-start.59
  876.1 8.7 collective-permute-start.60
  879.5 6.7 collective-permute-start.61
  884.8 16.6 %collective-permute-start.1 = (f32[8,2304]{1,0:T(8,128)}, f32[8,2304]{1,0:T(8,128)S(1)}, u32[]{:S(2)}, u32[]{:S(2)}) collective-permute-start(f32[8,2304]{1,0:T(8,128)} %get-tuple-element.160), channel_id=1, source_target_pairs={{0,2},{1,3},{2,4},{3,5},{4,6},{5,7},{6,8},{7,9},{8,10},{9,11},{10,... | collective-permute-start | bytes 221192
  886.1 18.7 %collective-permute-start.10 = (f32[8,2304]{1,0:T(8,128)}, f32[8,2304]{1,0:T(8,128)S(1)}, u32[]{:S(2)}, u32[]{:S(2)}) collective-permute-start(f32[8,2304]{1,0:T(8,128)} %get-tuple-element.160), channel_id=1, source_target_pairs={{0,11},{1,12},{2,13},{3,14},{4,15},{5,16},{6,17},{7,18},{8,19},{9,... | collective-permute-start | bytes 221192
  889.4 17.2 %collective-permute-start.11 = (f32[8,2304]{1,0:T(8,128)}, f32[8,2304]{1,0:T(8,128)S(1)}, u32[]{:S(2)}, u32[]{:S(2)}) collective-permute-start(f32[8,2304]{1,0:T(8,128)} %get-tuple-element.160), channel_id=1, source_target_pairs={{0,12},{1,13},{2,14},{3,15},{4,16},{5,17},{6,18},{7,19},{8,20},{9,... | collective-permute-start | bytes 221192
  893.4 17.6 %collective-permute-start.12 = (f32[8,2304]{1,0:T(8,128)}, f32[8,2304]{1,0:T(8,128)S(1)}, u32[]{:S(2)}, u32[]{:S(2)}) collective-permute-start(f32[8,2304]{1,0:T(8,128)} %get-tuple-element.160), channel_id=1, source_target_pairs={{0,13},{1,14},{2,15},{3,16},{4,17},{5,18},{6,19},{7,20},{8,21},{9,... | collective-permute-start | bytes 221192
  898.0 14.6 %collective-permute-start.13 = (f32[8,2304]{1,0:T(8,128)}, f32[8,2304]{1,0:T(8,128)S(1)}, u32[]{:S(2)}, u32[]{:S(2)}) collective-permute-start(f32[8,2304]{1,0:T(8,128)} %get-tuple-element.160), channel_id=1, source_target_pairs={{0,14},{1,15},{2,16},{3,17},{4,18},{5,19},{6,20},{7,21},{8,22},{9,... | collective-permute-start | bytes 221192
  901.5 13.5 %collective-permute-start.14 = (f32[8,2304]{1,0:T(8,128)}, f32[8,2304]{1,0:T(8,128)S(1)}, u32[]{:S(2)}, u32[]{:S(2)}) collective-permute-start(f32[8,2304]{1,0:T(8,128)} %get-tuple-element.160), channel_id=1, source_target_pairs={{0,15},{1,16},{2,17},{3,18},{4,19},{5,20},{6,21},{7,22},{8,23},{9,... | collective-permute-start | bytes 221192
  904.9 13.0 %collective-permute-start.15 = (f32[8,2304]{1,0:T(8,128)}, f32[8,2304]{1,0:T(8,128)S(1)}, u32[]{:S(2)}, u32[]{:S(2)}) collective-permute-start(f32[8,2304]{1,0:T(8,128)} %get-tuple-element.160), channel_id=1, source_target_pairs={{0,16},{1,17},{2,18},{3,19},{4,20},{5,21},{6,22},{7,23},{8,24},{9,... | collective-permute-start | bytes 221192
  906.6 14.0 %collective-permute-start.16 = (f32[8,2304]{1,0:T(8,128)}, f32[8,2304]{1,0:T(8,128)S(1)}, u32[]{:S(2)}, u32[]{:S(2)}) collective-permute-start(f32[8,2304]{1,0:T(8,128)} %get-tuple-element.160), channel_id=1, source_target_pairs={{0,17},{1,18},{2,19},{3,20},{4,21},{5,22},{6,23},{7,24},{8,25},{9,... | collective-permute-start | bytes 221192
  911.0 13.1 %collective-permute-start.17 = (f32[8,2304]{1,0:T(8,128)}, f32[8,2304]{1,0:T(8,128)S(1)}, u32[]{:S(2)}, u32[]{:S(2)}) collective-permute-start(f32[8,2304]{1,0:T(8,128)} %get-tuple-element.160), channel_id=1, source_target_pairs={{0,18},{1,19},{2,20},{3,21},{4,22},{5,23},{6,24},{7,25},{8,26},{9,... | collective-permute-start | bytes 221192
  912.7 12.8 %collective-permute-start.18 = (f32[8,2304]{1,0:T(8,128)}, f32[8,2304]{1,0:T(8,128)S(1)}, u32[]{:S(2)}, u32[]{:S(2)}) collective-permute-start(f32[8,2304]{1,0:T(8,128)} %get-tuple-element.160), channel_id=1, source_target_pairs={{0,19},{1,20},{2,21},{3,22},{4,23},{5,24},{6,25},{7,26},{8,27},{9,... | collective-permute-start | bytes 221192
  915.0 11.8 %collective-permute-start.19 = (f32[8,2304]{1,0:T(8,128)}, f32[8,2304]{1,0:T(8,128)S(1)}, u32[]{:S(2)}, u32[]{:S(2)}) collective-permute-start(f32[8,2304]{1,0:T(8,128)} %get-tuple-element.160), channel_id=1, source_target_pairs={{0,20},{1,21},{2,22},{3,23},{4,24},{5,25},{6,26},{7,27},{8,28},{9,... | collective-permute-start | bytes 221192
  917.9 10.2 collective-permute-start.2
  920.7 9.2 collective-permute-start.20
  924.1 7.1 collective-permute-start.21
  925.5 7.8 collective-permute-start.22
  926.8 11.1 %collective-permute-start.23 = (f32[8,2304]{1,0:T(8,128)}, f32[8,2304]{1,0:T(8,128)S(1)}, u32[]{:S(2)}, u32[]{:S(2)}) collective-permute-start(f32[8,2304]{1,0:T(8,128)} %get-tuple-element.160), channel_id=1, source_target_pairs={{0,24},{1,25},{2,26},{3,27},{4,28},{5,29},{6,30},{7,31},{8,32},{9,... | collective-permute-start | bytes 221192
  928.1 12.2 %collective-permute-start.24 = (f32[8,2304]{1,0:T(8,128)}, f32[8,2304]{1,0:T(8,128)S(1)}, u32[]{:S(2)}, u32[]{:S(2)}) collective-permute-start(f32[8,2304]{1,0:T(8,128)} %get-tuple-element.160), channel_id=1, source_target_pairs={{0,25},{1,26},{2,27},{3,28},{4,29},{5,30},{6,31},{7,32},{8,33},{9,... | collective-permute-start | bytes 221192
  929.9 12.4 %collective-permute-start.25 = (f32[8,2304]{1,0:T(8,128)}, f32[8,2304]{1,0:T(8,128)S(1)}, u32[]{:S(2)}, u32[]{:S(2)}) collective-permute-start(f32[8,2304]{1,0:T(8,128)} %get-tuple-element.160), channel_id=1, source_target_pairs={{0,26},{1,27},{2,28},{3,29},{4,30},{5,31},{6,32},{7,33},{8,34},{9,... | collective-permute-start | bytes 221192
  931.2 13.0 %collective-permute-start.26 = (f32[8,2304]{1,0:T(8,128)}, f32[8,2304]{1,0:T(8,128)S(1)}, u32[]{:S(2)}, u32[]{:S(2)}) collective-permute-start(f32[8,2304]{1,0:T(8,128)} %get-tuple-element.160), channel_id=1, source_target_pairs={{0,27},{1,28},{2,29},{3,30},{4,31},{5,32},{6,33},{7,34},{8,35},{9,... | collective-permute-start | bytes 221192
  933.3 12.9 %collective-permute-start.27 = (f32[8,2304]{1,0:T(8,128)}, f32[8,2304]{1,0:T(8,128)S(1)}, u32[]{:S(2)}, u32[]{:S(2)}) collective-permute-start(f32[8,2304]{1,0:T(8,128)} %get-tuple-element.160), channel_id=1, source_target_pairs={{0,28},{1,29},{2,30},{3,31},{4,32},{5,33},{6,34},{7,35},{8,36},{9,... | collective-permute-start | bytes 221192
  937.9 61.9 %collective-permute-start.28 = (f32[8,2304]{1,0:T(8,128)}, f32[8,2304]{1,0:T(8,128)}, u32[]{:S(2)}, u32[]{:S(2)}) collective-permute-start(f32[8,2304]{1,0:T(8,128)} %get-tuple-element.160), channel_id=1, source_target_pairs={{0,29},{1,30},{2,31},{3,32},{4,33},{5,34},{6,35},{7,36},{8,37},{9,... | collective-permute-start | bytes 221192
  940.4 62.0 %collective-permute-start.29 = (f32[8,2304]{1,0:T(8,128)}, f32[8,2304]{1,0:T(8,128)}, u32[]{:S(2)}, u32[]{:S(2)}) collective-permute-start(f32[8,2304]{1,0:T(8,128)} %get-tuple-element.160), channel_id=1, source_target_pairs={{0,30},{1,31},{2,32},{3,33},{4,34},{5,35},{6,36},{7,37},{8,38},{9,... | collective-permute-start | bytes 221192
  942.3 62.2 %collective-permute-start.3 = (f32[8,2304]{1,0:T(8,128)}, f32[8,2304]{1,0:T(8,128)}, u32[]{:S(2)}, u32[]{:S(2)}) collective-permute-start(f32[8,2304]{1,0:T(8,128)} %get-tuple-element.160), channel_id=1, source_target_pairs={{0,4},{1,5},{2,6},{3,7},{4,8},{5,9},{6,10},{7,11},{8,12},{9,13},{1... | collective-permute-start | bytes 221192
  944.2 63.6 %collective-permute-start.30 = (f32[8,2304]{1,0:T(8,128)}, f32[8,2304]{1,0:T(8,128)}, u32[]{:S(2)}, u32[]{:S(2)}) collective-permute-start(f32[8,2304]{1,0:T(8,128)} %get-tuple-element.160), channel_id=1, source_target_pairs={{0,31},{1,32},{2,33},{3,34},{4,35},{5,36},{6,37},{7,38},{8,39},{9,... | collective-permute-start | bytes 221192
  946.1 63.6 %collective-permute-start.4 = (f32[8,2304]{1,0:T(8,128)}, f32[8,2304]{1,0:T(8,128)}, u32[]{:S(2)}, u32[]{:S(2)}) collective-permute-start(f32[8,2304]{1,0:T(8,128)} %get-tuple-element.160), channel_id=1, source_target_pairs={{0,5},{1,6},{2,7},{3,8},{4,9},{5,10},{6,11},{7,12},{8,13},{9,14},{... | collective-permute-start | bytes 221192
  999.8 15.3 %collective-permute-start.5 = (f32[8,2304]{1,0:T(8,128)}, f32[8,2304]{1,0:T(8,128)}, u32[]{:S(2)}, u32[]{:S(2)}) collective-permute-start(f32[8,2304]{1,0:T(8,128)} %get-tuple-element.160), channel_id=1, source_target_pairs={{0,6},{1,7},{2,8},{3,9},{4,10},{5,11},{6,12},{7,13},{8,14},{9,15},... | collective-permute-start | bytes 221192
  1002.4 12.7 %collective-permute-start.6 = (f32[8,2304]{1,0:T(8,128)}, f32[8,2304]{1,0:T(8,128)}, u32[]{:S(2)}, u32[]{:S(2)}) collective-permute-start(f32[8,2304]{1,0:T(8,128)} %get-tuple-element.160), channel_id=1, source_target_pairs={{0,7},{1,8},{2,9},{3,10},{4,11},{5,12},{6,13},{7,14},{8,15},{9,16}... | collective-permute-start | bytes 221192
  1004.5 10.6 collective-permute-start.7
  1007.8 7.3 collective-permute-start.8
  (49 other events, 1443.9 us)
Sparse Core Ops, SparseCore 0:
  55.5 26.3 all-gather.1
  384.3 31.9 reduce-scatter.7
where the time goes:
time: 1090 us; the launch traced here: 1080 us
  blocking collectives  403 us (37%)
  local copies, waits for them, and re-layouts  204 us (19%)
  starting transfers between devices  178 us (16%)
  matrix products  175 us (16%)
  other arithmetic  78.9 us (7%)
  waiting for transfers between devices  22.3 us (2%)
  between operations  16 us (1%)
    unnamed x2, blocking collectives  378 us
    unnamed x65, starting transfers between devices  174 us
    unnamed x77, local copies, waits for them, and re-layouts  119 us
    dynamic_slice x96, local copies, waits for them, and re-layouts, block_pass(): lax.map(lambda group: head_pass(*group, key_mask), (to_heads(qkv[:, :widt...  51.1 us
    dot_general x12, matrix products, head_pass(): jnp.dot(prob_bf16, values_all, preferred_element_type=jnp.float32)  47.7 us
    div x12, other arithmetic, head_pass(): prob_exact = raw_weights / jnp.sum(raw_weights, axis=-1, keepdims=True)  38.1 us
    all_to_all x1, blocking collectives, shards(): lax.all_to_all(buffer.reshape(slides, CAP, width), 'slide', split_axis=0,...  25 us
    dot_general x12, matrix products, head_pass(): grad_p = jnp.dot(d_head, values_all.T, preferred_element_type=jnp.float32)  23.4 us
  transfers between devices with their start and end apart: 67, of which 2 were waited for; matrix products, arithmetic and copies ran while one was open for 7% of the time, Pallas kernels for 0%

commit v1 on v0

v1 whole, which is shorter than its diff:
```python
import functools

import jax
import jax.numpy as jnp
import numpy as np
from jax import lax
from jax.experimental import pallas as pl
from jax.experimental.pallas import tpu as pltpu
from jax.sharding import PartitionSpec as P

HEADS = 12
CAP = 48
RATE = 8
WIDTH = 768
SLOTS = 768
KEYS = 1536
BLOCK = 256
SIDE = 4
THIRD = 1024
MASKED = -1e30
BF16 = jnp.bfloat16
F32 = jnp.float32
MESH = pl.DeviceIdType.MESH
ORDERS = (("x", "y", "z"), ("y", "z", "x"), ("z", "x", "y"))
NT = (((1,), (1,)), ((), ()))


def embed_tiles(feats, norm_gain, w_embed):
    values = feats.astype(F32)
    center = jnp.mean(values, axis=-1, keepdims=True)
    spread = jnp.mean((values - center) ** 2, axis=-1, keepdims=True)
    normed = ((values - center) * lax.rsqrt(spread + 1e-06) * norm_gain).astype(BF16)
    return jnp.dot(normed, w_embed, preferred_element_type=F32).astype(BF16)


def place_tiles(embedded, targets, slides):
    one_hot = (targets[:, None] == jnp.arange(slides, dtype=jnp.int32)[None, :]).astype(jnp.int32)
    order_rank = jnp.sum((jnp.cumsum(one_hot, axis=0) - 1) * one_hot, axis=1)
    slot_index = targets * CAP + order_rank
    placing = (jnp.arange(slides * CAP, dtype=jnp.int32)[:, None] == slot_index[None, :]).astype(BF16)
    buffer = jnp.dot(placing, embedded, preferred_element_type=F32).astype(BF16)
    return (buffer, jnp.sum(one_hot, axis=0))


def row_orders():
    feature = np.arange(WIDTH)
    device, inner = feature // 6, feature % 6
    at = {"core": device % 2, "z": device // 2 % 4, "x": device // 8 % 4, "y": device // 32}
    places = [
        at["core"] * 384 + at[a] * 96 + at[b] * 24 + at[c] * 6 + inner for a, b, c in ORDERS
    ]
    return np.broadcast_to(np.stack(places)[:, None, :], (3, 8, WIDTH)).astype(np.int32)


def dot(a, b):
    return jnp.dot(a, b, preferred_element_type=F32)


def layer_kernel(
    x_ref, xd_ref, val_ref, cot_ref, wqkv_ref, wout_ref, place_ref, att_ref, g_ref,
    q_tok, k_tok, v_tok, do_tok, q_t, k_t, v_t, do_t, mg, o_t, dq_t, dq_tok, dkv,
    scores, prob, grad, perm, xp_t, op_t, filler,
):
    mg_val = val_ref[:SLOTS, :].astype(BF16)
    for c in range(6):
        cols = slice(c * 128, c * 128 + 128)
        mg[:, cols] = cot_ref[:, cols] * mg_val
    row = lax.broadcasted_iota(jnp.int32, (64, SLOTS), 0)
    filler[...] = jnp.where(row == 0, 1.0, 0.0).astype(BF16)

    @pl.loop(0, 3)
    def _(c):
        start = pl.multiple_of(c * BLOCK, BLOCK)
        cols = pl.ds(start, BLOCK)
        query = dot(x_ref[...], wqkv_ref[:, cols]).astype(BF16) * BF16(0.125)
        q_tok[:, cols] = query
        q_t[cols, :] = query.T
        for base, tok, turned in ((WIDTH, k_tok, k_t), (2 * WIDTH, v_tok, v_t)):
            w_cols = pl.ds(pl.multiple_of(start + base, BLOCK), BLOCK)
            for first, rows_ref in ((0, x_ref), (SLOTS, xd_ref)):
                part = dot(rows_ref[...], wqkv_ref[:, w_cols]).astype(BF16)
                tok[first : first + SLOTS, cols] = part
                turned[cols, first : first + SLOTS] = part.T
        d_heads = lax.dot_general(mg[...], wout_ref[cols, :], NT, preferred_element_type=F32).astype(BF16)
        do_tok[:, cols] = d_heads
        do_t[cols, :] = d_heads.T

    @pl.loop(0, HEADS // 2)
    def _(pair):
        lanes = pl.ds(pl.multiple_of(pair * 128, 128), 128)
        k2, v2 = k_tok[:, lanes], v_tok[:, lanes]
        bias = jnp.where(val_ref[...] > 0.5, 0.0, MASKED).astype(BF16)
        lane = lax.broadcasted_iota(jnp.int32, (KEYS, 128), 1)
        keys, q_rows, do_rows, zeros = [], [], [], jnp.zeros((64, SLOTS), BF16)
        for a in range(2):
            rows = pl.ds(pl.multiple_of(pair * 128 + a * 64, 64), 64)
            own = lane < 64 if a == 0 else lane >= 64
            keys.append(jnp.where(own, k2, bias))
            q_part, do_part = q_t[rows, :], do_t[rows, :]
            halves = (q_part, filler[...]) if a == 0 else (filler[...], q_part)
            q_rows.append(jnp.concatenate(halves, axis=0))
            halves = (do_part, zeros) if a == 0 else (zeros, do_part)
            do_rows.append(jnp.concatenate(halves, axis=0))

        for step in range(6):
            a, block = step // 3, step % 3
            cols = slice(block * BLOCK, block * BLOCK + BLOCK)
            rows = pl.ds(pl.multiple_of(pair * 128 + a * 64, 64), 64)
            slot = step % 2
            out_cols = slice(a * SLOTS + block * BLOCK, a * SLOTS + block * BLOCK + BLOCK)
            s = dot(keys[a], q_rows[a][:, cols])
            peak = jnp.max(s, axis=0, keepdims=True)
            raw = jnp.exp(s - peak)
            scores[slot] = raw
            inverse = 1.0 / jnp.sum(raw, axis=0, keepdims=True)
            p = (scores[slot] * inverse).astype(BF16)
            prob[:, out_cols] = p
            out = dot(v_t[rows, :], p).astype(BF16)
            o_t[rows, cols] = out
            delta = jnp.sum(do_t[rows, cols].astype(F32) * out.astype(F32), axis=0, keepdims=True)
            grad_p = dot(v2, do_rows[a][:, cols])
            ds = (scores[slot] * inverse * (grad_p - delta)).astype(BF16)
            grad[:, out_cols] = ds
            dq_t[rows, cols] = (dot(k_t[rows, :], ds) * 0.125).astype(BF16)

        lane_q = lax.broadcasted_iota(jnp.int32, (SLOTS, 128), 1)
        q2, do2 = q_tok[:, lanes], do_tok[:, lanes]
        nothing = jnp.zeros((SLOTS, 128), BF16)
        q_cat = jnp.concatenate([jnp.where(lane_q < 64, q2, nothing), jnp.where(lane_q < 64, nothing, q2)], axis=0)
        do_cat = jnp.concatenate([jnp.where(lane_q < 64, do2, nothing), jnp.where(lane_q < 64, nothing, do2)], axis=0)
        dkv[:, lanes] = dot(grad[...], q_cat).astype(BF16)
        dkv[:, pl.ds(pl.multiple_of(pair * 128 + WIDTH, 128), 128)] = dot(prob[...], do_cat).astype(BF16)
        dq_tok[:, lanes] = dq_t[lanes, :].T

    @pl.loop(0, 3)
    def _(c):
        cols = pl.ds(pl.multiple_of(c * BLOCK, BLOCK), BLOCK)
        mixed = x_ref[:, cols].astype(F32) + lax.dot_general(
            o_t[...], wout_ref[:, cols], (((0,), (0,)), ((), ())), preferred_element_type=F32
        )
        att_ref[:, cols] = (mixed * val_ref[:SLOTS, :1]).astype(BF16)

    for t in range(3):
        place = place_ref[t][:1, :]
        perm[...] = (lax.broadcasted_iota(jnp.int32, (WIDTH, WIDTH), 0) == place).astype(BF16)

        @pl.loop(0, 3)
        def _(c):
            start = pl.multiple_of(c * BLOCK, BLOCK)
            rows = pl.ds(start, BLOCK)
            xp_t[:, rows] = lax.dot_general(perm[...], x_ref[rows, :], NT, preferred_element_type=F32).astype(BF16)
            far = pl.ds(pl.multiple_of(start + SLOTS, BLOCK), BLOCK)
            xp_t[:, far] = lax.dot_general(perm[...], xd_ref[rows, :], NT, preferred_element_type=F32).astype(BF16)
            if t == 2:
                op_t[:, rows] = dot(perm[...], o_t[:, rows]).astype(BF16)

        for n in range(4):
            chunk = t * 4 + n
            cols = slice(n * BLOCK, n * BLOCK + BLOCK)
            if chunk < 3:
                part = dot(xp_t[:, :SLOTS], dq_tok[:, chunk * BLOCK : chunk * BLOCK + BLOCK])
            elif chunk < 9:
                part = dot(xp_t[...], dkv[:, chunk * BLOCK - WIDTH : chunk * BLOCK - WIDTH + BLOCK])
            else:
                part = dot(op_t[...], mg[:, chunk * BLOCK - 2304 : chunk * BLOCK - 2304 + BLOCK])
            g_ref[t, :, cols] = part.astype(BF16)


def layer(x, xd, val, cot, w_qkv, w_out):
    tall, wide = (KEYS, WIDTH), (WIDTH, KEYS)
    square = (SLOTS, WIDTH)
    vmem = pl.BlockSpec(memory_space=pltpu.VMEM)
    shapes = [
        square, tall, tall, square, square, wide, wide, square, square, square, square, square, (KEYS, KEYS),
    ]
    scratch = [pltpu.VMEM(s, BF16) for s in shapes]
    scratch += [
        pltpu.VMEM((2, KEYS, BLOCK), F32),
        pltpu.VMEM((KEYS, KEYS), BF16),
        pltpu.VMEM((KEYS, KEYS), BF16),
        pltpu.VMEM(square, BF16),
        pltpu.VMEM(wide, BF16),
        pltpu.VMEM(square, BF16),
        pltpu.VMEM((64, SLOTS), BF16),
    ]
    return pl.pallas_call(
        layer_kernel,
        out_shape=(
            jax.ShapeDtypeStruct((SLOTS, WIDTH), BF16),
            jax.ShapeDtypeStruct((3, WIDTH, THIRD), BF16),
        ),
        in_specs=[vmem] * 7,
        out_specs=(vmem, vmem),
        scratch_shapes=scratch,
        compiler_params=pltpu.CompilerParams(vmem_limit_bytes=62 * 1024 * 1024),
        cost_estimate=pl.CostEstimate(flops=28_000_000_000, bytes_accessed=16_000_000, transcendentals=14_000_000),
        name="layer",
    )(x, xd, val, cot, w_qkv, w_out, jnp.asarray(row_orders()))


def sum_kernel(factor, g_ref, oq_ref, oo_ref, half, pair_sum, from_a, owned, from_b, spread, from_c,
               send0, recv0, send_a, recv_a, send_b, recv_b, send_c, recv_c):
    slide, seq = lax.axis_index("slide"), lax.axis_index("seq")
    at = {"y": slide // SIDE, "x": slide % SIDE, "z": seq // 2}
    core = seq % 2

    def peer(axis, distance):
        moved = dict(at)
        moved[axis] = lax.rem(at[axis] + distance, SIDE)
        return moved[axis], (moved["y"] * SIDE + moved["x"], moved["z"] * 2 + core)

    sibling = (slide, at["z"] * 2 + 1 - core)
    barrier = pltpu.get_barrier_semaphore()
    others = [sibling] + [peer(axis, d)[1] for axis in "xyz" for d in (1, 2, 3)]
    for other in others:
        pl.semaphore_signal(barrier, inc=1, device_id=other, device_id_type=MESH)
    pl.semaphore_wait(barrier, len(others))

    def remote(src, dst, send, recv, device):
        copy = pltpu.make_async_remote_copy(
            src_ref=src, dst_ref=dst, send_sem=send, recv_sem=recv, device_id=device, device_id_type=MESH
        )
        copy.start()
        return copy

    started = []
    own_half = pl.multiple_of(core * 384, 384)
    its_half = pl.multiple_of((1 - core) * 384, 384)
    zero = [
        remote(g_ref.at[t, pl.ds(its_half, 384), :], half.at[t], send0.at[t], recv0.at[t], sibling) for t in range(3)
    ]
    stage_a = []
    for t in range(3):
        zero[t].wait_recv()
        pair_sum[t] = (g_ref[t, pl.ds(own_half, 384), :].astype(F32) + half[t].astype(F32)).astype(BF16)
        row = []
        for d in (2, 1, 3):
            there, device = peer(ORDERS[t][0], d)
            src = pair_sum.at[t, pl.ds(pl.multiple_of(there * 96, 96), 96), :]
            row.append(remote(src, from_a.at[t, d - 1], send_a.at[t, d - 1], recv_a.at[t, d - 1], device))
        stage_a.append(row)
    stage_b = []
    for t in range(3):
        mine = pl.multiple_of(at[ORDERS[t][0]] * 96, 96)
        total = g_ref[t, pl.ds(pl.multiple_of(own_half + mine, 96), 96), :].astype(F32)
        total = total + half[t, pl.ds(mine, 96), :].astype(F32)
        for copy in stage_a[t]:
            copy.wait_recv()
        for d in range(3):
            total = total + from_a[t, d].astype(F32)
        owned[t] = total
        row = []
        for d in (2, 1, 3):
            there, device = peer(ORDERS[t][1], d)
            src = owned.at[t, pl.ds(pl.multiple_of(there * 24, 24), 24), :]
            row.append(remote(src, from_b.at[t, d - 1], send_b.at[t, d - 1], recv_b.at[t, d - 1], device))
        stage_b.append(row)
    stage_c = []
    for t in range(3):
        mine = pl.multiple_of(at[ORDERS[t][1]] * 24, 24)
        total = owned[t, pl.ds(mine, 24), :]
        for copy in stage_b[t]:
            copy.wait_recv()
        for d in range(3):
            total = total + from_b[t, d]
        for c in range(SIDE):
            spread[t, c, :6, :] = total[c * 6 : c * 6 + 6]
            spread[t, c, 6:, :] = jnp.zeros((2, THIRD), F32)
        row = []
        for d in (2, 1, 3):
            there, device = peer(ORDERS[t][2], d)
            row.append(remote(spread.at[t, there], from_c.at[t, d - 1], send_c.at[t, d - 1], recv_c.at[t, d - 1], device))
        stage_c.append(row)
    for t in range(3):
        total = spread[t, at[ORDERS[t][2]]]
        for copy in stage_c[t]:
            copy.wait_recv()
        for d in range(3):
            total = total + from_c[t, d]
        total = total[:6] * factor
        if t < 2:
            oq_ref[:, t * THIRD : t * THIRD + THIRD] = total
        else:
            oq_ref[:, 2 * THIRD :] = total[:, :BLOCK]
            oo_ref[...] = total[:, BLOCK:]
    for copy in zero:
        copy.wait_send()
    for stage in (stage_a, stage_b, stage_c):
        for row in stage:
            for copy in row:
                copy.wait_send()


def sum_gradients(g, factor):
    vmem = pl.BlockSpec(memory_space=pltpu.VMEM)
    return pl.pallas_call(
        functools.partial(sum_kernel, factor),
        out_shape=(jax.ShapeDtypeStruct((6, 3 * WIDTH), F32), jax.ShapeDtypeStruct((6, WIDTH), F32)),
        in_specs=[vmem],
        out_specs=(vmem, vmem),
        scratch_shapes=[
            pltpu.VMEM((3, 384, THIRD), BF16),
            pltpu.VMEM((3, 384, THIRD), BF16),
            pltpu.VMEM((3, 3, 96, THIRD), BF16),
            pltpu.VMEM((3, 96, THIRD), F32),
            pltpu.VMEM((3, 3, 24, THIRD), F32),
            pltpu.VMEM((3, SIDE, 8, THIRD), F32),
            pltpu.VMEM((3, 3, 8, THIRD), F32),
            pltpu.SemaphoreType.DMA((3,)),
            pltpu.SemaphoreType.DMA((3,)),
        ] + [pltpu.SemaphoreType.DMA((3, 3))] * 6,
        compiler_params=pltpu.CompilerParams(
            collective_id=1, has_side_effects=True, vmem_limit_bytes=48 * 1024 * 1024
        ),
        cost_estimate=pl.CostEstimate(flops=10_000_000, bytes_accessed=5_000_000, transcendentals=0),
        name="sum_gradients",
    )(g)


def shards(tile_feats, norm_gain, w_embed, slide_of_tile, w_qkv, w_out, cotangent):
    width = w_out.shape[0]
    slides = lax.axis_size("slide")
    blocks = lax.axis_size("seq")
    embedded = embed_tiles(tile_feats, norm_gain, w_embed)
    buffer, counts = place_tiles(embedded, slide_of_tile[:, 0], slides)
    received, arrived = (
        lax.all_to_all(
            buffer.reshape(slides, CAP, width), "slide", split_axis=0, concat_axis=0, tiled=True
        ),
        lax.all_to_all(counts.reshape(slides, 1), "slide", split_axis=0, concat_axis=0, tiled=True),
    )
    rows_in = received.reshape(slides * CAP, width)
    valid = (jnp.arange(CAP, dtype=jnp.int32)[None, :] < arrived).astype(F32).reshape(slides * CAP)
    rows_far, valid_far = (
        lax.all_gather(rows_in[::RATE], "seq", axis=0, tiled=True),
        lax.all_gather(valid[::RATE].astype(BF16), "seq", axis=0, tiled=True),
    )
    val = jnp.broadcast_to(jnp.concatenate([valid, valid_far.astype(F32)])[:, None], (KEYS, 128))
    output, partial = layer(rows_in, rows_far, val, cotangent[0], w_qkv, w_out)
    factor = (slides * blocks * rows_in.shape[0]) ** (-0.5)
    grad_qkv, grad_out = sum_gradients(partial, factor)
    return (output[None], grad_qkv, grad_out)


def solution(mesh):
    return jax.shard_map(
        shards,
        mesh=mesh,
        in_specs=(
            P(("slide", "seq"), None),
            P(),
            P(),
            P(("slide", "seq"), None),
            P(),
            P(),
            P("slide", "seq", None),
        ),
        out_specs=(P("slide", "seq", None), P(("slide", "seq"), None), P(("slide", "seq"), None)),
        check_vma=False,
    )
```

time: 1090 us -> 214 us (0.20); the launches traced: 1080 us -> 214 us
  blocking collectives: 403 us -> 41 us
  local copies, waits for them, and re-layouts: 204 us -> 8.46 us
  starting transfers between devices: 178 us -> 3.51 us
  matrix products: 175 us -> 3.5 us
  Pallas kernels: 0 us -> 133 us
  other arithmetic: 78.9 us -> 4.89 us
  waiting for transfers between devices: 22.3 us -> 5.05 us
    unnamed x2 -> x1, blocking collectives: 378 us -> 16.2 us
    unnamed x65 -> x0, starting transfers between devices: 174 us -> none
    dot_general x80 -> x1, matrix products: 175 us -> 3.5 us  [place_tiles(): buffer = jnp.dot(placing, embedded, preferred_element_type=F32).astype(BF16)]
    pallas_call x0 -> x2, Pallas kernels: none -> 133 us  [the longest x1 106 us: layer(): pl.pallas_call(layer_kernel, out_shape=(jax.ShapeDtypeStruct((SLOTS, WIDT...]
    unnamed x77 -> x17, local copies, waits for them, and re-layouts: 119 us -> 4.43 us
    dynamic_slice x96 -> x0, local copies, waits for them, and re-layouts: 51.1 us -> none  [block_pass(): lax.map(lambda group: head_pass(*group, key_mask), (to_heads(qkv[:, :widt...]
    div x12 -> x0, other arithmetic: 38.1 us -> none  [head_pass(): prob_exact = raw_weights / jnp.sum(raw_weights, axis=-1, keepdims=True)]
    reduce_sum x25 -> x1, other arithmetic: 24.5 us -> 0.15 us  [place_tiles(): return (buffer, jnp.sum(one_hot, axis=0))]
  transfers between devices with their start and end apart: 67 -> 2, of which waited for: 2 -> 1; matrix products, arithmetic and copies ran while one was open for 7% -> 1% of each run, Pallas kernels for 0% -> 0%
where the time goes in v1:
time: 214 us
  Pallas kernels  133 us (62%)
  blocking collectives  41 us (19%)
  between operations  14.8 us (7%)
  local copies, waits for them, and re-layouts  8.46 us (4%)
  waiting for transfers between devices  5.05 us (2%)
  other arithmetic  4.89 us (2%)
  starting transfers between devices  3.51 us (2%)
  matrix products  3.5 us (2%)
    pallas_call x1, Pallas kernels, layer(): pl.pallas_call(layer_kernel, out_shape=(jax.ShapeDtypeStruct((SLOTS, WIDT...  106 us
    pallas_call x1, Pallas kernels, sum_gradients(): pl.pallas_call(functools.partial(sum_kernel, factor), out_shape=(jax.Shap...  26.8 us
    all_to_all x1, blocking collectives, shards(): lax.all_to_all(buffer.reshape(slides, CAP, width), 'slide', split_axis=0,...  24.8 us
    unnamed x1, blocking collectives  16.2 us
    all_to_all x1, waiting for transfers between devices, shards(): lax.all_to_all(counts.reshape(slides, 1), 'slide', split_axis=0, concat_a...  5.02 us
    unnamed x17, local copies, waits for them, and re-layouts  4.43 us
  transfers between devices with their start and end apart: 2, of which 1 were waited for; matrix products, arithmetic and copies ran while one was open for 1% of the time, Pallas kernels for 0%

profile of v1, /device:TPU:1, one launch (start us, length us, event | category | flops | bytes accessed | tf_op | source)
XLA Modules:
  0.0 213.9 jit_solution(10069447619690987876)
XLA Ops:
  7.2 0.0 copy-start.1
  7.2 0.0 copy-start.3
  7.2 0.0 copy-start.4
  7.2 0.0 all-gather.2.cloned.1.call-start
  7.2 1.6 convert_reduce_fusion
  8.8 1.7 fusion.2
  10.6 0.0 copy-done.3
  10.6 0.9 reduce-window.6
  11.5 0.2 slice_reduce_fusion
  11.7 0.2 convert_reduce_fusion.1
  11.9 0.0 copy-done.1
  11.9 0.0 copy-done.4
  11.9 3.5 %convolution_convert_fusion = bf16[768,768]{1,0:T(8,128)(2,1)S(1)} fusion(bf16[1536,768]{1,0:T(8,128)(2,1)} %param.10, bf16[384,1536]{1,0:T(8,128)(2,1)S(1)} %copy-done.1, f32[1536]{0:T(1024)S(1)} %copy-done.4, f32[384]{0:T(512)S(1)} %add_rsqrt_fusion, f32[384]{0:T(512)S(1)} %broadcast_multiply_fusion, s32[384]{0:T(512)S(1)} %multiply_add_fusion), kind=kOutput, calls=%fused_computation.7 | convolution fusion | flops 1363083264 | bytes 4729344 | tf_op jit(solution)/shard_map/dot_general | solution.py:41
  15.4 0.0 copy-start.5
  15.4 24.8 %all_to_all.14 = bf16[16,48,768]{2,1,0:T(8,128)(2,1)S(1)} all-to-all(bf16[16,48,768]{2,1,0:T(8,128)(2,1)S(1)} %bitcast.26), channel_id=1, replica_groups=mesh['slide'=16,'seq'=8] {'slide'}, dimensions={0} | all-to-all | bytes 2359296 | tf_op jit(solution)/shard_map/all_to_all | solution.py:327
  40.2 0.0 copy-start.2
  40.2 1.7 slice.15
  42.0 0.0 all-gather.2.cloned.1.call-update
  42.0 0.7 copy.15
  42.7 3.5 %all-to-all-start.1 = ((s32[16,1,1]{2,1,0:T(1,128)}), s32[16,1,1]{2,1,0:T(1,128)S(1)}, u32[]{:S(2)}, u32[]{:S(2)}) async-start(s32[16,1,1]{2,1,0:T(1,128)} %copy.15), calls=%async_computation.1 | async-start | bytes 16384 | tf_op jit(solution)/shard_map/all_to_all | solution.py:330
  46.1 0.0 copy-done.5
  46.2 0.6 dynamic-slice
  47.4 5.0 %all-to-all-done.1 = s32[16,1,1]{2,1,0:T(1,128)S(1)} async-done(((s32[16,1,1]{2,1,0:T(1,128)}), s32[16,1,1]{2,1,0:T(1,128)S(1)}, u32[]{:S(2)}, u32[]{:S(2)}) %all-to-all-start.1) | async-done | bytes 96 | tf_op jit(solution)/shard_map/all_to_all | solution.py:330
  52.4 0.4 reduce.3
  52.8 0.1 fusion.15
  52.9 0.1 reshape.66
  53.0 0.2 slice.16
  53.2 0.2 dynamic-update-slice
  53.4 16.2 %all-reduce = bf16[768]{0:T(1024)(128)(2,1)S(1)} all-reduce(bf16[768]{0:T(1024)(128)(2,1)S(1)} %dynamic-update-slice), channel_id=1, replica_groups=mesh['slide'=16,'seq'=8] {'seq'}, use_global_device_ids=true, to_apply=%add | all-reduce | flops 768 | bytes 3072
  69.6 0.0 all-gather.2.cloned.1.call-done.xd_ref
  69.6 1.1 broadcast_in_dim.4.val_ref
  70.8 0.0 copy-done.2
  70.8 105.9 %layer.1 = (bf16[768,768]{1,0:T(8,128)(2,1)}, bf16[3,768,1024]{2,1,0:T(8,128)(2,1)}) custom-call(bf16[768,768]{1,0:T(8,128)(2,1)} %bitcast.25, bf16[768,768]{1,0:T(8,128)(2,1)} %all-gather.2.cloned.1.call-done.xd_ref, f32[1536,128]{1,0:T(8,128)} %broadcast_in_dim.4.val_ref, bf16[768,768]{1,0:T(8,128)(2,1)} %bitcast.30, bf16[768,2304]{1,0:T(8,128)(2,1)} %wqkv_ref.1, ...), custom_call_target="tpu_custom_call" | custom-call | flops 28000000000 | bytes 16000000 | tf_op jit(solution)/shard_map/layer/pallas_call | solution.py:186
  176.7 0.0 copy-start
  176.7 2.3 %copy-done = bf16[3,768,1024]{2,1,0:T(8,128)(2,1)S(1)} copy-done((bf16[3,768,1024]{2,1,0:T(8,128)(2,1)S(1)}, bf16[3,768,1024]{2,1,0:T(8,128)(2,1)}, u32[]{:S(2)}) %copy-start) | copy-done | bytes 4718616
  179.0 26.8 %sum_gradients.1 = (f32[6,2304]{1,0:T(8,128)S(1)}, f32[6,768]{1,0:T(8,128)S(1)}) custom-call(bf16[3,768,1024]{2,1,0:T(8,128)(2,1)S(1)} %copy-done), custom_call_target="tpu_custom_call" | custom-call | flops 10000000 | bytes 5000000 | tf_op jit(solution)/shard_map/sum_gradients/pallas_call | solution.py:296
  205.8 0.6 copy.21
  206.4 0.6 copy.22
  (10 shorter events, 0.1 us)
Async XLA Ops:
  7.2 4.7 %copy-start.1 = (bf16[384,1536]{1,0:T(8,128)(2,1)S(1)}, bf16[384,1536]{1,0:T(8,128)(2,1)}, u32[]{:S(2)}) copy-start(bf16[384,1536]{1,0:T(8,128)(2,1)} %param.8) | copy-start | bytes 3538948
  7.2 3.4 %copy-start.3 = (s32[384,1]{0,1:T(1,128)S(1)}, s32[384,1]{0,1:T(1,128)}, u32[]{:S(2)}) copy-start(s32[384,1]{0,1:T(1,128)} %param.11) | copy-start | bytes 4612
  7.2 4.7 %copy-start.4 = (f32[1536]{0:T(1024)S(1)}, f32[1536]{0:T(1024)}, u32[]{:S(2)}) copy-start(f32[1536]{0:T(1024)} %param.9) | copy-start | bytes 18436
  7.2 62.4 %all-gather.2.cloned.1.call-start = ((), (), s32[]{:S(2)}) async-start(), calls=%async_computation.2 | async-start | bytes 1327104 | tf_op jit(solution)/shard_map/all_gather | solution.py:335
  15.4 30.7 %copy-start.5 = (u32[128]{0:T(128)S(1)}, u32[128]{0:T(128)}, u32[]{:S(2)}) copy-start(u32[128]{0:T(128)} %constant.25) | copy-start | bytes 1540
  40.2 30.6 %copy-start.2 = (bf16[16,48,768]{2,1,0:T(8,128)(2,1)}, bf16[16,48,768]{2,1,0:T(8,128)(2,1)S(1)}, u32[]{:S(2)}) copy-start(bf16[16,48,768]{2,1,0:T(8,128)(2,1)S(1)} %all_to_all.14) | copy-start | bytes 3538948
  42.7 9.7 %all-to-all-start.1 = ((s32[16,1,1]{2,1,0:T(1,128)}), s32[16,1,1]{2,1,0:T(1,128)S(1)}, u32[]{:S(2)}, u32[]{:S(2)}) async-start(s32[16,1,1]{2,1,0:T(1,128)} %copy.15), calls=%async_computation.1 | async-start | bytes 16384 | tf_op jit(solution)/shard_map/all_to_all | solution.py:330
  176.7 2.3 %copy-start = (bf16[3,768,1024]{2,1,0:T(8,128)(2,1)S(1)}, bf16[3,768,1024]{2,1,0:T(8,128)(2,1)}, u32[]{:S(2)}) copy-start(bf16[3,768,1024]{2,1,0:T(8,128)(2,1)} %get-tuple-element.8.g_ref) | copy-start | bytes 14155780
Sparse Core Ops, SparseCore 0:
  42.1 24.3 all-gather.1

commit v2 on v1

v2 whole, which is shorter than its diff:
```python
import functools

import jax
import jax.numpy as jnp
import numpy as np
from jax import lax
from jax.experimental import pallas as pl
from jax.experimental.pallas import tpu as pltpu
from jax.sharding import PartitionSpec as P

HEADS = 12
CAP = 48
RATE = 8
WIDTH = 768
WIDE = 1536
TILES = 384
SLOTS = 768
KEYS = 1536
BLOCK = 256
PART = 512
SIDE = 4
THIRD = 1024
MASKED = -1e30
BF16 = jnp.bfloat16
F32 = jnp.float32
MESH = pl.DeviceIdType.MESH
ORDERS = (("x", "y", "z"), ("y", "z", "x"), ("z", "x", "y"))
NT = (((1,), (1,)), ((), ()))


def front_kernel(
    feats_ref, gain_ref, we_ref, target_ref, x_ref, xd_ref, near_ref, far_ref,
    normed, embedded, placed, tally, near_all, own_far, mine16,
    send_x, recv_x, send_n, recv_n, send_f, recv_f, send_z, recv_z, send_s, recv_s, local,
):
    slide, seq = lax.axis_index("slide"), lax.axis_index("seq")
    z, core = seq // 2, seq % 2
    slides = [(lax.rem(slide + k, 16), seq) for k in range(1, 16)]
    blocks = [(slide, lax.rem(seq + k, 8)) for k in range(1, 8)]
    barrier = pltpu.get_barrier_semaphore()
    for device in slides + blocks:
        pl.semaphore_signal(barrier, inc=1, device_id=device, device_id_type=MESH)

    def remote(src, dst, send, recv, device):
        copy = pltpu.make_async_remote_copy(
            src_ref=src, dst_ref=dst, send_sem=send, recv_sem=recv, device_id=device, device_id_type=MESH
        )
        copy.start()
        return copy

    target = target_ref[...]
    named = lax.broadcasted_iota(jnp.int32, (16, TILES), 0) == target
    one_hot = jnp.where(named, 1.0, 0.0)
    earlier = (
        lax.broadcasted_iota(jnp.int32, (TILES, TILES), 0) < lax.broadcasted_iota(jnp.int32, (TILES, TILES), 1)
    ).astype(BF16)
    before = dot(one_hot.astype(BF16), earlier)
    rank = jnp.sum(one_hot * before, axis=0, keepdims=True)
    slot = target * CAP + rank.astype(jnp.int32)
    placing = (lax.broadcasted_iota(jnp.int32, (SLOTS, TILES), 0) == slot).astype(BF16)
    total = jnp.sum(one_hot, axis=1, keepdims=True)
    for d in range(16):
        tally[d] = jnp.broadcast_to(total[d : d + 1], (8, 128))

    @pl.loop(0, 4)
    def _(c):
        rows = pl.ds(pl.multiple_of(c * 96, 96), 96)
        values = feats_ref[rows, :].astype(F32)
        center = jnp.mean(values, axis=-1, keepdims=True)
        moved = values - center
        spread = jnp.mean(moved * moved, axis=-1, keepdims=True)
        normed[rows, :] = (moved * lax.rsqrt(spread + 1e-06) * gain_ref[...]).astype(BF16)

    pl.semaphore_wait(barrier, 22)
    near_copies = [
        remote(tally.at[dev[0]], near_all.at[slide], send_n.at[k], recv_n.at[k], dev) for k, dev in enumerate(slides)
    ]
    near_all[slide] = tally[slide]
    x_copies = []
    for half in range(2):
        cols = slice(half * 384, half * 384 + 384)
        embedded[...] = dot(normed[...], we_ref[:, cols]).astype(BF16)
        placed[:, cols] = dot(placing, embedded[...]).astype(BF16)
        for k in (7, 8, 6, 9, 5, 10, 4, 11, 3, 12, 2, 13, 1, 14, 0):
            dev = slides[k]
            src = placed.at[pl.ds(pl.multiple_of(dev[0] * CAP, CAP), CAP), cols]
            dst = x_ref.at[pl.ds(pl.multiple_of(slide * CAP, CAP), CAP), cols]
            x_copies.append(remote(src, dst, send_x.at[half, k], recv_x.at[half, k], dev))
    own = pl.ds(pl.multiple_of(slide * CAP, CAP), CAP)
    x_ref[own, :] = placed[own, :]

    for copy in near_copies:
        copy.wait_recv()
    for i in range(16):
        mine16[i : i + 1, :] = near_all[i][:1]
    near_ref[...] = mine16[...]
    far_copies = [remote(mine16, far_ref.at[seq], send_f.at[k], recv_f.at[k], dev) for k, dev in enumerate(blocks)]
    far_ref[seq] = mine16[...]

    row = lax.broadcasted_iota(jnp.int32, (96, SLOTS), 0)
    pick = lax.broadcasted_iota(jnp.int32, (96, SLOTS), 1) == (row % 16) * CAP + (row // 16) * RATE
    pick = pick.astype(BF16)
    for copy in x_copies:
        copy.wait_recv()
    rows = dot(pick, x_ref[...]).astype(BF16)
    for m in range(6):
        own_far[m] = rows[m * 16 : m * 16 + 16]

    sibling = (slide, z * 2 + 1 - core)
    up = (slide, lax.rem(z + 1, SIDE) * 2 + core)
    down = (slide, lax.rem(z + 3, SIDE) * 2 + core)
    to_up = remote(own_far, xd_ref.at[:, seq], send_z.at[0], recv_z.at[0], up)
    to_down = remote(own_far, xd_ref.at[:, seq], send_z.at[1], recv_z.at[1], down)
    to_side = [remote(own_far, xd_ref.at[:, seq], send_s.at[0], recv_s.at[0], sibling)]
    keep = pltpu.make_async_copy(own_far, xd_ref.at[:, seq], local)
    keep.start()
    to_up.wait_recv()
    relay_up = remote(xd_ref.at[pl.ds(0, 3), down[1]], xd_ref.at[pl.ds(0, 3), down[1]], send_z.at[2], recv_z.at[2], up)
    to_side.append(remote(xd_ref.at[:, down[1]], xd_ref.at[:, down[1]], send_s.at[1], recv_s.at[1], sibling))
    to_down.wait_recv()
    relay_down = remote(xd_ref.at[pl.ds(3, 3), up[1]], xd_ref.at[pl.ds(3, 3), up[1]], send_z.at[3], recv_z.at[3], down)
    to_side.append(remote(xd_ref.at[:, up[1]], xd_ref.at[:, up[1]], send_s.at[2], recv_s.at[2], sibling))
    relay_up.wait_recv()
    relay_down.wait_recv()
    across = lax.rem(z + 2, SIDE) * 2 + core
    to_side.append(remote(xd_ref.at[:, across], xd_ref.at[:, across], send_s.at[3], recv_s.at[3], sibling))
    for copy in to_side + far_copies:
        copy.wait_recv()
    keep.wait()
    for copy in to_side + far_copies + near_copies + x_copies + [to_up, to_down, relay_up, relay_down]:
        copy.wait_send()


def front(feats, gain, w_embed, target):
    vmem = pl.BlockSpec(memory_space=pltpu.VMEM)
    dma = pltpu.SemaphoreType.DMA
    return pl.pallas_call(
        front_kernel,
        out_shape=(
            jax.ShapeDtypeStruct((SLOTS, WIDTH), BF16),
            jax.ShapeDtypeStruct((6, 8, 16, WIDTH), BF16),
            jax.ShapeDtypeStruct((16, 128), F32),
            jax.ShapeDtypeStruct((8, 16, 128), F32),
        ),
        in_specs=[vmem] * 4,
        out_specs=(vmem,) * 4,
        scratch_shapes=[
            pltpu.VMEM((TILES, WIDE), BF16),
            pltpu.VMEM((TILES, WIDTH // 2), BF16),
            pltpu.VMEM((SLOTS, WIDTH), BF16),
            pltpu.VMEM((16, 8, 128), F32),
            pltpu.VMEM((16, 8, 128), F32),
            pltpu.VMEM((6, 16, WIDTH), BF16),
            pltpu.VMEM((16, 128), F32),
            dma((2, 15)), dma((2, 15)), dma((15,)), dma((15,)), dma((7,)), dma((7,)),
            dma((4,)), dma((4,)), dma((4,)), dma((4,)), dma,
        ],
        compiler_params=pltpu.CompilerParams(
            collective_id=2, has_side_effects=True, vmem_limit_bytes=40 * 1024 * 1024
        ),
        cost_estimate=pl.CostEstimate(flops=2_000_000_000, bytes_accessed=8_000_000, transcendentals=0),
        name="front",
    )(feats, gain, w_embed, target)


def row_orders():
    feature = np.arange(WIDTH)
    device, inner = feature // 6, feature % 6
    at = {"core": device % 2, "z": device // 2 % 4, "x": device // 8 % 4, "y": device // 32}
    places = [
        at["core"] * 384 + at[a] * 96 + at[b] * 24 + at[c] * 6 + inner for a, b, c in ORDERS
    ]
    return np.broadcast_to(np.stack(places)[:, None, :], (3, 8, WIDTH)).astype(np.int32)


def dot(a, b):
    return jnp.dot(a, b, preferred_element_type=F32)


def layer_kernel(
    x_ref, xd_ref, near_ref, far_ref, cot_ref, wqkv_ref, wout_ref, place_ref, att_ref, g_ref,
    val, bias, q_tok, k_tok, v_tok, do_tok, q_t, k_t, v_t, do_t, x_t, mg, o_t, dq_t, dq_tok, dkv,
    score_0, score_1, grad_p, prob_0, prob_1, grad_0, grad_1, key_0, key_1, q_0, q_1, do_0, do_1,
    qc_0, qc_1, dc_0, dc_1,
):
    scores, prob, grad = (score_0, score_1), (prob_0, prob_1), (grad_0, grad_1)
    keys, q_rows, do_rows = (key_0, key_1), (q_0, q_1), (do_0, do_1)
    q_cat, do_cat = (qc_0, qc_1), (dc_0, dc_1)

    place_in = lax.broadcasted_iota(jnp.int32, (CAP, 128), 0).astype(F32)
    for i in range(16):
        val[i * CAP : i * CAP + CAP, :] = jnp.where(place_in < near_ref[i : i + 1, :], 1.0, 0.0)
    for m in range(6):
        for j in range(8):
            first = SLOTS + m * 128 + j * 16
            val[first : first + 16, :] = jnp.where(far_ref[j] > m * RATE, 1.0, 0.0)
    bias[...] = jnp.where(val[...] > 0.5, 0.0, MASKED).astype(BF16)
    mg_val = val[:SLOTS, :].astype(BF16)
    for c in range(6):
        cols = slice(c * 128, c * 128 + 128)
        mg[:, cols] = cot_ref[:, cols] * mg_val
    row = lax.broadcasted_iota(jnp.int32, (64, SLOTS), 0)
    filler = jnp.where(row == 0, 1.0, 0.0).astype(BF16)
    zeros = jnp.zeros((64, SLOTS), BF16)
    q_0[64:, :], q_1[:64, :] = filler, filler
    do_0[64:, :], do_1[:64, :] = zeros, zeros

    @pl.loop(0, 3)
    def _(c):
        start = pl.multiple_of(c * BLOCK, BLOCK)
        cols = pl.ds(start, BLOCK)
        query = dot(x_ref[...], wqkv_ref[:, cols]).astype(BF16) * BF16(0.125)
        q_tok[:, cols] = query
        q_t[cols, :] = query.T
        for first, rows_ref in ((0, x_ref), (SLOTS, xd_ref)):
            x_t[cols, first : first + SLOTS] = rows_ref[:, cols].T
        for base, tok, turned in ((WIDTH, k_tok, k_t), (2 * WIDTH, v_tok, v_t)):
            w_cols = pl.ds(pl.multiple_of(start + base, BLOCK), BLOCK)
            for first, rows_ref in ((0, x_ref), (SLOTS, xd_ref)):
                part = dot(rows_ref[...], wqkv_ref[:, w_cols]).astype(BF16)
                tok[first : first + SLOTS, cols] = part
                turned[cols, first : first + SLOTS] = part.T
        d_heads = lax.dot_general(mg[...], wout_ref[cols, :], NT, preferred_element_type=F32).astype(BF16)
        do_tok[:, cols] = d_heads
        do_t[cols, :] = d_heads.T

    def lanes_of(pair):
        return pl.ds(pl.multiple_of(pair * 128, 128), 128)

    def close_keys(pair, a, third):
        rows = slice(third * PART, third * PART + PART)
        mine = lax.broadcasted_iota(jnp.int32, (PART, 128), 1) // 64 == a
        for offset, left, right in ((0, grad[a], q_cat[a]), (WIDTH, prob[a], do_cat[a])):
            lanes = pl.ds(pl.multiple_of(pair * 128 + offset, 128), 128)
            part = dot(left[rows, :], right[...]).astype(BF16)
            dkv[rows, lanes] = jnp.where(mine, part, dkv[rows, lanes])

    @pl.loop(0, HEADS // 2)
    def _(pair):
        lanes = lanes_of(pair)
        before = lax.max(pair - 1, 0)
        lane = lax.broadcasted_iota(jnp.int32, (KEYS, 128), 1)
        lane_q = lax.broadcasted_iota(jnp.int32, (SLOTS, 128), 1)
        nothing = jnp.zeros((SLOTS, 128), BF16)

        def head_rows(a):
            return pl.ds(pl.multiple_of(pair * 128 + a * 64, 64), 64)

        def open_head(a):
            own = slice(a * 64, a * 64 + 64)
            keys[a][...] = jnp.where(lane // 64 == a, k_tok[:, lanes], bias[...])
            q_rows[a][own, :] = q_t[head_rows(a), :]
            do_rows[a][own, :] = do_t[head_rows(a), :]

        def score_part(step, part):
            a, block = step // 3, step % 3
            rows = slice(part * PART, part * PART + PART)
            cols = slice(block * BLOCK, block * BLOCK + BLOCK)
            s = dot(keys[a][rows, :], q_rows[a][:, cols])
            scores[step % 2][rows, :] = s
            return jnp.max(s, axis=0, keepdims=True)

        def top(parts):
            return jnp.maximum(jnp.maximum(parts[0], parts[1]), parts[2])

        open_head(0)
        peak = top([score_part(0, part) for part in range(3)])
        open_head(1)
        for step in range(6):
            a, block = step // 3, step % 3
            cols = slice(block * BLOCK, block * BLOCK + BLOCK)
            score = scores[step % 2]
            peaks, sums = [], []
            for part in range(3):
                rows = slice(part * PART, part * PART + PART)
                if step < 5:
                    peaks.append(score_part(step + 1, part))
                raw = jnp.exp(score[rows, :] - peak)
                score[rows, :] = raw
                sums.append(jnp.sum(raw, axis=0, keepdims=True))
            inverse = 1.0 / (sums[0] + sums[1] + sums[2])
            for part in range(3):
                rows = slice(part * PART, part * PART + PART)
                grad_p[rows, :] = dot(v_tok[rows, lanes], do_rows[a][:, cols])
                p = score[rows, :] * inverse
                score[rows, :] = p
                prob[a][rows, cols] = p.astype(BF16)
            out = dot(v_t[head_rows(a), :], prob[a][:, cols]).astype(BF16)
            o_t[head_rows(a), cols] = out
            if a == 0:
                close_keys(before, 1, block)
            else:
                close_keys(pair, 0, block)
            delta = jnp.sum(do_t[head_rows(a), cols].astype(F32) * out.astype(F32), axis=0, keepdims=True)
            for part in range(3):
                rows = slice(part * PART, part * PART + PART)
                grad[a][rows, cols] = (score[rows, :] * (grad_p[rows, :] - delta)).astype(BF16)
            dq_t[head_rows(a), cols] = (dot(k_t[head_rows(a), :], grad[a][:, cols]) * 0.125).astype(BF16)
            if step < 5:
                peak = top(peaks)
            if block == 2:
                half = lane_q // 64 == a
                q_cat[a][...] = jnp.where(half, q_tok[:, lanes], nothing)
                do_cat[a][...] = jnp.where(half, do_tok[:, lanes], nothing)
        dq_tok[:, lanes] = dq_t[lanes, :].T

    for third in range(3):
        close_keys(HEADS // 2 - 1, 1, third)

    @pl.loop(0, 3)
    def _(c):
        cols = pl.ds(pl.multiple_of(c * BLOCK, BLOCK), BLOCK)
        mixed = x_ref[:, cols].astype(F32) + lax.dot_general(
            o_t[...], wout_ref[:, cols], (((0,), (0,)), ((), ())), preferred_element_type=F32
        )
        att_ref[:, cols] = (mixed * val[:SLOTS, :1]).astype(BF16)

    perm = prob_0
    for t in range(3):
        place = place_ref[t][:1, :]
        perm[:WIDTH, :] = (lax.broadcasted_iota(jnp.int32, (WIDTH, WIDTH), 0) == place).astype(BF16)
        for n in range(4):
            chunk = t * 4 + n
            cols = slice(n * BLOCK, n * BLOCK + BLOCK)
            if chunk < 3:
                part = dot(x_t[:, :SLOTS], dq_tok[:, chunk * BLOCK : chunk * BLOCK + BLOCK])
            elif chunk < 9:
                part = dot(x_t[...], dkv[:, chunk * BLOCK - WIDTH : chunk * BLOCK - WIDTH + BLOCK])
            else:
                part = dot(o_t[...], mg[:, chunk * BLOCK - 2304 : chunk * BLOCK - 2304 + BLOCK])
            g_ref[t, :, cols] = dot(perm[:WIDTH, :], part.astype(BF16)).astype(BF16)


def layer(x, xd, near, far, cot, w_qkv, w_out):
    tall, wide = (KEYS, WIDTH), (WIDTH, KEYS)
    square = (SLOTS, WIDTH)
    vmem = pl.BlockSpec(memory_space=pltpu.VMEM)
    scratch = [pltpu.VMEM((KEYS, 128), F32), pltpu.VMEM((KEYS, 128), BF16)]
    shapes = [
        square, tall, tall, square, square, wide, wide, square, wide, square, square, square, square, (KEYS, KEYS),
    ]
    scratch += [pltpu.VMEM(s, BF16) for s in shapes]
    scratch += [pltpu.VMEM((KEYS, BLOCK), F32)] * 3
    scratch += [pltpu.VMEM(tall, BF16)] * 4
    scratch += [pltpu.VMEM((KEYS, 128), BF16)] * 2
    scratch += [pltpu.VMEM((128, SLOTS), BF16)] * 4
    scratch += [pltpu.VMEM((SLOTS, 128), BF16)] * 4
    return pl.pallas_call(
        layer_kernel,
        out_shape=(
            jax.ShapeDtypeStruct((SLOTS, WIDTH), BF16),
            jax.ShapeDtypeStruct((3, WIDTH, THIRD), BF16),
        ),
        in_specs=[vmem] * 8,
        out_specs=(vmem, vmem),
        scratch_shapes=scratch,
        compiler_params=pltpu.CompilerParams(vmem_limit_bytes=62 * 1024 * 1024),
        cost_estimate=pl.CostEstimate(flops=28_000_000_000, bytes_accessed=16_000_000, transcendentals=14_000_000),
        name="layer",
    )(x, xd, near, far, cot, w_qkv, w_out, jnp.asarray(row_orders()))


def sum_kernel(factor, g_ref, oq_ref, oo_ref, half, pair_sum, from_a, owned, from_b, spread, from_c,
               send0, recv0, send_a, recv_a, send_b, recv_b, send_c, recv_c):
    slide, seq = lax.axis_index("slide"), lax.axis_index("seq")
    at = {"y": slide // SIDE, "x": slide % SIDE, "z": seq // 2}
    core = seq % 2

    def peer(axis, distance):
        moved = dict(at)
        moved[axis] = lax.rem(at[axis] + distance, SIDE)
        return moved[axis], (moved["y"] * SIDE + moved["x"], moved["z"] * 2 + core)

    sibling = (slide, at["z"] * 2 + 1 - core)
    barrier = pltpu.get_barrier_semaphore()
    others = [sibling] + [peer(axis, d)[1] for axis in "xyz" for d in (1, 2, 3)]
    for other in others:
        pl.semaphore_signal(barrier, inc=1, device_id=other, device_id_type=MESH)
    pl.semaphore_wait(barrier, len(others))

    def remote(src, dst, send, recv, device):
        copy = pltpu.make_async_remote_copy(
            src_ref=src, dst_ref=dst, send_sem=send, recv_sem=recv, device_id=device, device_id_type=MESH
        )
        copy.start()
        return copy

    started = []
    own_half = pl.multiple_of(core * 384, 384)
    its_half = pl.multiple_of((1 - core) * 384, 384)
    zero = [
        remote(g_ref.at[t, pl.ds(its_half, 384), :], half.at[t], send0.at[t], recv0.at[t], sibling) for t in range(3)
    ]
    stage_a = []
    for t in range(3):
        zero[t].wait_recv()
        pair_sum[t] = (g_ref[t, pl.ds(own_half, 384), :].astype(F32) + half[t].astype(F32)).astype(BF16)
        row = []
        for d in (2, 1, 3):
            there, device = peer(ORDERS[t][0], d)
            src = pair_sum.at[t, pl.ds(pl.multiple_of(there * 96, 96), 96), :]
            row.append(remote(src, from_a.at[t, d - 1], send_a.at[t, d - 1], recv_a.at[t, d - 1], device))
        stage_a.append(row)
    stage_b = []
    for t in range(3):
        mine = pl.multiple_of(at[ORDERS[t][0]] * 96, 96)
        total = g_ref[t, pl.ds(pl.multiple_of(own_half + mine, 96), 96), :].astype(F32)
        total = total + half[t, pl.ds(mine, 96), :].astype(F32)
        for copy in stage_a[t]:
            copy.wait_recv()
        for d in range(3):
            total = total + from_a[t, d].astype(F32)
        owned[t] = total
        row = []
        for d in (2, 1, 3):
            there, device = peer(ORDERS[t][1], d)
            src = owned.at[t, pl.ds(pl.multiple_of(there * 24, 24), 24), :]
            row.append(remote(src, from_b.at[t, d - 1], send_b.at[t, d - 1], recv_b.at[t, d - 1], device))
        stage_b.append(row)
    stage_c = []
    for t in range(3):
        mine = pl.multiple_of(at[ORDERS[t][1]] * 24, 24)
        total = owned[t, pl.ds(mine, 24), :]
        for copy in stage_b[t]:
            copy.wait_recv()
        for d in range(3):
            total = total + from_b[t, d]
        for c in range(SIDE):
            spread[t, c, :6, :] = total[c * 6 : c * 6 + 6]
            spread[t, c, 6:, :] = jnp.zeros((2, THIRD), F32)
        row = []
        for d in (2, 1, 3):
            there, device = peer(ORDERS[t][2], d)
            row.append(remote(spread.at[t, there], from_c.at[t, d - 1], send_c.at[t, d - 1], recv_c.at[t, d - 1], device))
        stage_c.append(row)
    for t in range(3):
        total = spread[t, at[ORDERS[t][2]]]
        for copy in stage_c[t]:
            copy.wait_recv()
        for d in range(3):
            total = total + from_c[t, d]
        total = total[:6] * factor
        if t < 2:
            oq_ref[:, t * THIRD : t * THIRD + THIRD] = total
        else:
            oq_ref[:, 2 * THIRD :] = total[:, :BLOCK]
            oo_ref[...] = total[:, BLOCK:]
    for copy in zero:
        copy.wait_send()
    for stage in (stage_a, stage_b, stage_c):
        for row in stage:
            for copy in row:
                copy.wait_send()


def sum_gradients(g, factor):
    vmem = pl.BlockSpec(memory_space=pltpu.VMEM)
    return pl.pallas_call(
        functools.partial(sum_kernel, factor),
        out_shape=(jax.ShapeDtypeStruct((6, 3 * WIDTH), F32), jax.ShapeDtypeStruct((6, WIDTH), F32)),
        in_specs=[vmem],
        out_specs=(vmem, vmem),
        scratch_shapes=[
            pltpu.VMEM((3, 384, THIRD), BF16),
            pltpu.VMEM((3, 384, THIRD), BF16),
            pltpu.VMEM((3, 3, 96, THIRD), BF16),
            pltpu.VMEM((3, 96, THIRD), F32),
            pltpu.VMEM((3, 3, 24, THIRD), F32),
            pltpu.VMEM((3, SIDE, 8, THIRD), F32),
            pltpu.VMEM((3, 3, 8, THIRD), F32),
            pltpu.SemaphoreType.DMA((3,)),
            pltpu.SemaphoreType.DMA((3,)),
        ] + [pltpu.SemaphoreType.DMA((3, 3))] * 6,
        compiler_params=pltpu.CompilerParams(
            collective_id=1, has_side_effects=True, vmem_limit_bytes=48 * 1024 * 1024
        ),
        cost_estimate=pl.CostEstimate(flops=10_000_000, bytes_accessed=5_000_000, transcendentals=0),
        name="sum_gradients",
    )(g)


def shards(tile_feats, norm_gain, w_embed, slide_of_tile, w_qkv, w_out, cotangent):
    x, xd, near, far = front(tile_feats, norm_gain.reshape(1, WIDE), w_embed, slide_of_tile.reshape(1, TILES))
    output, partial = layer(x, xd.reshape(SLOTS, WIDTH), near, far, cotangent[0], w_qkv, w_out)
    factor = (lax.axis_size("slide") * lax.axis_size("seq") * SLOTS) ** (-0.5)
    grad_qkv, grad_out = sum_gradients(partial, factor)
    return (output[None], grad_qkv, grad_out)


def solution(mesh):
    return jax.shard_map(
        shards,
        mesh=mesh,
        in_specs=(
            P(("slide", "seq"), None),
            P(),
            P(),
            P(("slide", "seq"), None),
            P(),
            P(),
            P("slide", "seq", None),
        ),
        out_specs=(P("slide", "seq", None), P(("slide", "seq"), None), P(("slide", "seq"), None)),
        check_vma=False,
    )
```

time: 214 us -> 168 us (0.79)
  blocking collectives: 41 us -> 0 us
  Pallas kernels: 133 us -> 156 us
  between operations: 14.8 us -> 0.66 us
  waiting for transfers between devices: 5.05 us -> 0 us
  other arithmetic: 4.89 us -> 0 us
  starting transfers between devices: 3.51 us -> 0 us
  matrix products: 3.5 us -> 0 us
  local copies, waits for them, and re-layouts: 8.46 us -> 11.2 us
    pallas_call x0 -> x1, Pallas kernels: none -> 35.7 us  [front(): pl.pallas_call(front_kernel, out_shape=(jax.ShapeDtypeStruct((SLOTS, WIDT...]
    all_to_all x1 -> x0, blocking collectives: 24.8 us -> none  [shards(): lax.all_to_all(buffer.reshape(slides, CAP, width), 'slide', split_axis=0,...]
    unnamed x1 -> x0, blocking collectives: 16.2 us -> none
    pallas_call x1, Pallas kernels: 106 us -> 90.9 us  [layer(): pl.pallas_call(layer_kernel, out_shape=(jax.ShapeDtypeStruct((SLOTS, WIDT...]
    unnamed x17 -> x18, local copies, waits for them, and re-layouts: 4.43 us -> 10.5 us
    all_to_all x1 -> x0, waiting for transfers between devices: 5.02 us -> none  [shards(): lax.all_to_all(counts.reshape(slides, 1), 'slide', split_axis=0, concat_a...]
    dot_general x1 -> x0, matrix products: 3.5 us -> none  [place_tiles(): buffer = jnp.dot(placing, embedded, preferred_element_type=F32).astype(BF16)]
    all_to_all x1 -> x0, starting transfers between devices: 3.47 us -> none  [shards(): lax.all_to_all(counts.reshape(slides, 1), 'slide', split_axis=0, concat_a...]
  transfers between devices with their start and end apart: 2 -> 0, of which waited for: 1 -> 0; matrix products, arithmetic and copies ran while one was open for 1% -> 0% of each run, Pallas kernels for 0% -> 0%
where the time goes in v2:
time: 168 us
  Pallas kernels  156 us (93%)
  local copies, waits for them, and re-layouts  11.2 us (7%)
    pallas_call x1, Pallas kernels, layer(): pl.pallas_call(layer_kernel, out_shape=(jax.ShapeDtypeStruct((SLOTS, WIDT...  90.9 us
    pallas_call x1, Pallas kernels, front(): pl.pallas_call(front_kernel, out_shape=(jax.ShapeDtypeStruct((SLOTS, WIDT...  35.7 us
    pallas_call x1, Pallas kernels, sum_gradients(): pl.pallas_call(functools.partial(sum_kernel, factor), out_shape=(jax.Shap...  29.5 us
    unnamed x18, local copies, waits for them, and re-layouts  10.5 us

profile of v2, /device:TPU:1, one launch (start us, length us, event | category | flops | bytes accessed | tf_op | source)
XLA Modules:
  0.0 168.0 jit_solution(4773009295817197257)
XLA Ops:
  0.6 0.7 reshape.15.gain_ref
  1.3 0.0 copy-start.1
  1.3 1.7 copy-done.1
  3.0 0.0 copy-start.2
  3.0 1.3 copy-done.2
  4.3 0.0 copy-start.3
  4.3 0.7 copy-done.3
  5.0 35.7 %front.1 = (bf16[768,768]{1,0:T(8,128)(2,1)S(1)}, bf16[6,8,16,768]{3,2,1,0:T(8,128)(2,1)S(1)}, f32[16,128]{1,0:T(8,128)S(1)}, f32[8,16,128]{2,1,0:T(8,128)S(1)}) custom-call(bf16[384,1536]{1,0:T(8,128)(2,1)S(1)} %copy-done.2, f32[1,1536]{1,0:T(1,128)S(1)} %reshape.15.gain_ref, bf16[1536,768]{1,0:T(8,128)(2,1)S(1)} %copy-done.1, s32[1,384]{1,0:T(1,128)S(1)} %bitcast.4), custom_call_target="tpu_custom_call" | custom-call | flops 2000000000 | bytes 8000000 | tf_op jit(solution)/shard_map/front/pallas_call | solution.py:137
  40.6 0.0 copy-start.4
  40.6 1.0 copy-done.4
  41.7 0.0 copy-start.5
  41.7 1.1 copy-done.5
  42.7 0.0 copy-start.6
  42.7 0.6 copy-done.6
  43.4 0.0 copy-start.7
  43.4 0.6 copy-done.7
  44.0 90.9 %layer.1 = (bf16[768,768]{1,0:T(8,128)(2,1)}, bf16[3,768,1024]{2,1,0:T(8,128)(2,1)}) custom-call(bf16[768,768]{1,0:T(8,128)(2,1)} %copy-done.5, bf16[768,768]{1,0:T(8,128)(2,1)} %bitcast.5, f32[16,128]{1,0:T(8,128)} %copy-done.7, f32[8,16,128]{2,1,0:T(8,128)} %copy-done.6, bf16[768,768]{1,0:T(8,128)(2,1)} %bitcast.6, bf16[768,2304]{1,0:T(8,128)(2,1)} %wqkv_ref.1, ...), custom_call_target="tpu_custom_call" | custom-call | flops 28000000000 | bytes 16000000 | tf_op jit(solution)/shard_map/layer/pallas_call | solution.py:348
  134.9 0.0 copy-start
  134.9 2.3 %copy-done = bf16[3,768,1024]{2,1,0:T(8,128)(2,1)S(1)} copy-done((bf16[3,768,1024]{2,1,0:T(8,128)(2,1)S(1)}, bf16[3,768,1024]{2,1,0:T(8,128)(2,1)}, u32[]{:S(2)}) %copy-start) | copy-done | bytes 4718616
  137.2 29.5 %sum_gradients.1 = (f32[6,2304]{1,0:T(8,128)S(1)}, f32[6,768]{1,0:T(8,128)S(1)}) custom-call(bf16[3,768,1024]{2,1,0:T(8,128)(2,1)S(1)} %copy-done), custom_call_target="tpu_custom_call" | custom-call | flops 10000000 | bytes 5000000 | tf_op jit(solution)/shard_map/sum_gradients/pallas_call | solution.py:458
  166.7 0.6 copy.13
  167.4 0.6 copy.14
Async XLA Ops:
  1.3 1.7 copy-start.1
  3.0 1.3 copy-start.2
  4.3 0.7 copy-start.3
  40.6 1.0 copy-start.4
  41.7 1.1 copy-start.5
  42.7 0.6 copy-start.6
  43.4 0.6 copy-start.7
  134.9 2.3 %copy-start = (bf16[3,768,1024]{2,1,0:T(8,128)(2,1)S(1)}, bf16[3,768,1024]{2,1,0:T(8,128)(2,1)}, u32[]{:S(2)}) copy-start(bf16[3,768,1024]{2,1,0:T(8,128)(2,1)} %get-tuple-element.16.g_ref) | copy-start | bytes 14155780

commit v3 on v0

v3 whole, which is shorter than its diff:
```python
import functools

import jax
import jax.numpy as jnp
import numpy as np
from jax import lax
from jax.experimental import pallas as pl
from jax.experimental.pallas import tpu as pltpu
from jax.sharding import PartitionSpec as P

HEADS = 12
CAP = 48
RATE = 8
WIDTH = 768
WIDE = 1536
TILES = 384
SLOTS = 768
KEYS = 1536
BLOCK = 256
PART = 512
SIDE = 4
MASKED = -1e30
BF16 = jnp.bfloat16
F32 = jnp.float32
MESH = pl.DeviceIdType.MESH
ORDERS = (("x", "y", "z"), ("y", "z", "x"), ("z", "x", "y"))
NT = (((1,), (1,)), ((), ()))


def row_orders():
    feature = np.arange(WIDTH)
    device, inner = feature // 6, feature % 6
    at = {"core": device % 2, "z": device // 2 % 4, "x": device // 8 % 4, "y": device // 32}
    places = [
        at["core"] * 384 + at[a] * 96 + at[b] * 24 + at[c] * 6 + inner for a, b, c in ORDERS
    ]
    return np.broadcast_to(np.stack(places)[:, None, :], (3, 8, WIDTH)).astype(np.int32)


def dot(a, b):
    return jnp.dot(a, b, preferred_element_type=F32)


def whole_kernel(
    factor,
    feats_ref, gain_ref, we_ref, target_ref, cot_ref, wqkv_ref, wout_ref, place_ref,
    att_ref, oq_ref, oo_ref,
    x, xd, val, bias, q_tok, k_tok, v_tok, do_tok, q_t, k_t, v_t, do_t, x_t, mg, o_t, wout,
    dq_t, dq_round, dkv, score_0, score_1, grad_p, prob_0, prob_1, grad_0, grad_1,
    key_0, key_1, q_0, q_1, do_0, do_1, qc_0, qc_1, dc_0, dc_1, perm,
    tally, near_all, near, far, own_far,
    g, half, pair_sum, from_a, owned, from_b, spread, from_c,
    load, send_x, recv_x, send_n, recv_n, send_f, recv_f, send_z, recv_z, send_s, recv_s,
    send0, recv0, send_a, recv_a, send_b, recv_b, send_c, recv_c,
):
    scores, prob, grad = (score_0, score_1), (prob_0, prob_1), (grad_0, grad_1)
    keys, q_rows, do_rows = (key_0, key_1), (q_0, q_1), (do_0, do_1)
    q_cat, do_cat = (qc_0, qc_1), (dc_0, dc_1)
    slide, seq = lax.axis_index("slide"), lax.axis_index("seq")
    at = {"y": slide // SIDE, "x": slide % SIDE, "z": seq // 2}
    z, core = at["z"], seq % 2
    sibling = (slide, z * 2 + 1 - core)
    slides = [(lax.rem(slide + k, 16), seq) for k in range(1, 16)]
    blocks = [(slide, lax.rem(seq + k, 8)) for k in range(1, 8)]

    barrier = pltpu.get_barrier_semaphore()
    for device in slides + blocks:
        pl.semaphore_signal(barrier, inc=1, device_id=device, device_id_type=MESH)

    def remote(src, dst, send, recv, device):
        return pltpu.make_async_remote_copy(
            src_ref=src, dst_ref=dst, send_sem=send, recv_sem=recv, device_id=device, device_id_type=MESH
        )

    def begin(*args):
        copy = remote(*args)
        copy.start()
        return copy

    feats, normed, placed, w_e, w_q, w_k, w_v = (
        grad_0.at[:SLOTS], grad_1.at[:SLOTS], grad_1.at[SLOTS:], prob_1,
        prob_0.at[:SLOTS], prob_0.at[SLOTS:], grad_0.at[SLOTS:],
    )
    sources = [
        (feats_ref.at[:, :WIDTH], feats.at[:TILES]), (feats_ref.at[:, WIDTH:], feats.at[TILES:]),
        (we_ref, w_e), (cot_ref, mg), (wout_ref, wout),
        (wqkv_ref.at[:, :WIDTH], w_q), (wqkv_ref.at[:, WIDTH : 2 * WIDTH], w_k), (wqkv_ref.at[:, 2 * WIDTH :], w_v),
    ]
    loads = [pltpu.make_async_copy(src, dst, load.at[n]) for n, (src, dst) in enumerate(sources)]
    for copy in loads:
        copy.start()

    target = target_ref[...]
    named = lax.broadcasted_iota(jnp.int32, (16, TILES), 0) == target
    one_hot = jnp.where(named, 1.0, 0.0)
    earlier = (
        lax.broadcasted_iota(jnp.int32, (TILES, TILES), 0) < lax.broadcasted_iota(jnp.int32, (TILES, TILES), 1)
    ).astype(BF16)
    before_it = dot(one_hot.astype(BF16), earlier)
    rank = jnp.sum(one_hot * before_it, axis=0, keepdims=True)
    slot = target * CAP + rank.astype(jnp.int32)
    placing = x_t.at[:, :TILES]
    placing[...] = (lax.broadcasted_iota(jnp.int32, (SLOTS, TILES), 0) == slot).astype(BF16)
    total = jnp.sum(one_hot, axis=1, keepdims=True)
    for d in range(16):
        tally[d] = jnp.broadcast_to(total[d : d + 1], (8, 128))
    loads[0].wait()
    loads[1].wait()

    @pl.loop(0, 4)
    def _(c):
        low = pl.ds(pl.multiple_of(c * 96, 96), 96)
        high = pl.ds(pl.multiple_of(c * 96 + TILES, 96), 96)
        values = [feats[low, :].astype(F32), feats[high, :].astype(F32)]
        center = sum(jnp.sum(v, axis=-1, keepdims=True) for v in values) * (1.0 / WIDE)
        moved = [v - center for v in values]
        spread_sq = sum(jnp.sum(v * v, axis=-1, keepdims=True) for v in moved) * (1.0 / WIDE)
        scale = lax.rsqrt(spread_sq + 1e-06)
        normed[low, :] = (moved[0] * scale * gain_ref[:, :WIDTH]).astype(BF16)
        normed[high, :] = (moved[1] * scale * gain_ref[:, WIDTH:]).astype(BF16)

    pl.semaphore_wait(barrier, 22)
    near_copies = [
        begin(tally.at[dev[0]], near_all.at[slide], send_n.at[k], recv_n.at[k], dev) for k, dev in enumerate(slides)
    ]
    near_all[slide] = tally[slide]
    loads[2].wait()
    x_copies = []
    for part in range(2):
        cols = slice(part * 384, part * 384 + 384)
        embedded = dot(normed[:TILES, :], w_e[:WIDTH, cols]) + dot(normed[TILES:, :], w_e[WIDTH:, cols])
        o_t[:TILES, cols] = embedded.astype(BF16)
        placed[:, cols] = dot(placing[...], o_t[:TILES, cols]).astype(BF16)
        for k in (7, 8, 6, 9, 5, 10, 4, 11, 3, 12, 2, 13, 1, 14, 0):
            dev = slides[k]
            src = placed.at[pl.ds(pl.multiple_of(dev[0] * CAP, CAP), CAP), cols]
            dst = x.at[pl.ds(pl.multiple_of(slide * CAP, CAP), CAP), cols]
            x_copies.append(begin(src, dst, send_x.at[part, k], recv_x.at[part, k], dev))
    own = pl.ds(pl.multiple_of(slide * CAP, CAP), CAP)
    x[own, :] = placed[own, :]

    for copy in near_copies:
        copy.wait_recv()
    for i in range(16):
        near[i : i + 1, :] = near_all[i][:1]
    far_copies = [begin(near, far.at[seq], send_f.at[k], recv_f.at[k], dev) for k, dev in enumerate(blocks)]
    far[seq] = near[...]
    place_in = lax.broadcasted_iota(jnp.int32, (CAP, 128), 0).astype(F32)
    for i in range(16):
        val[i * CAP : i * CAP + CAP, :] = jnp.where(place_in < near[i : i + 1, :], 1.0, 0.0)
    for t in range(3):
        perm[t] = (lax.broadcasted_iota(jnp.int32, (WIDTH, WIDTH), 0) == place_ref[t][:1, :]).astype(BF16)
    row = lax.broadcasted_iota(jnp.int32, (64, SLOTS), 0)
    filler = jnp.where(row == 0, 1.0, 0.0).astype(BF16)
    zeros = jnp.zeros((64, SLOTS), BF16)
    q_0[64:, :], q_1[:64, :] = filler, filler
    do_0[64:, :], do_1[:64, :] = zeros, zeros
    for copy in loads[3:]:
        copy.wait()
    mg_val = val[:SLOTS, :].astype(BF16)
    for c in range(6):
        cols = slice(c * 128, c * 128 + 128)
        mg[:, cols] = mg[:, cols] * mg_val

    @pl.loop(0, 3)
    def _(c):
        cols = pl.ds(pl.multiple_of(c * BLOCK, BLOCK), BLOCK)
        d_heads = lax.dot_general(mg[...], wout[cols, :], NT, preferred_element_type=F32).astype(BF16)
        do_tok[:, cols] = d_heads
        do_t[cols, :] = d_heads.T

    row = lax.broadcasted_iota(jnp.int32, (96, SLOTS), 0)
    pick = lax.broadcasted_iota(jnp.int32, (96, SLOTS), 1) == (row % 16) * CAP + (row // 16) * RATE
    pick = pick.astype(BF16)
    for copy in x_copies:
        copy.wait_recv()
    rows = dot(pick, x[...]).astype(BF16)
    for m in range(6):
        own_far[m] = rows[m * 16 : m * 16 + 16]

    up = (slide, lax.rem(z + 1, SIDE) * 2 + core)
    down = (slide, lax.rem(z + 3, SIDE) * 2 + core)
    across = lax.rem(z + 2, SIDE) * 2 + core
    to_up = begin(own_far, xd.at[:, seq], send_z.at[0], recv_z.at[0], up)
    to_down = begin(own_far, xd.at[:, seq], send_z.at[1], recv_z.at[1], down)
    to_side = [begin(own_far, xd.at[:, seq], send_s.at[0], recv_s.at[0], sibling)]
    xd[:, seq] = own_far[...]

    def project(first, rows_of):
        @pl.loop(0, 3)
        def _(c):
            cols = pl.ds(pl.multiple_of(c * BLOCK, BLOCK), BLOCK)
            x_t[cols, first : first + SLOTS] = rows_of(cols).T
            for w, tok, turned in ((w_k, k_tok, k_t), (w_v, v_tok, v_t)):
                part = dot(rows_of(slice(None)), w[:, cols]).astype(BF16)
                tok[first : first + SLOTS, cols] = part
                turned[cols, first : first + SLOTS] = part.T

    @pl.loop(0, 3)
    def _(c):
        cols = pl.ds(pl.multiple_of(c * BLOCK, BLOCK), BLOCK)
        query = dot(x[...], w_q[:, cols]).astype(BF16) * BF16(0.125)
        q_tok[:, cols] = query
        q_t[cols, :] = query.T

    to_up.wait_recv()
    relay_up = begin(xd.at[pl.ds(0, 3), down[1]], xd.at[pl.ds(0, 3), down[1]], send_z.at[2], recv_z.at[2], up)
    to_side.append(begin(xd.at[:, down[1]], xd.at[:, down[1]], send_s.at[1], recv_s.at[1], sibling))
    to_down.wait_recv()
    relay_down = begin(xd.at[pl.ds(3, 3), up[1]], xd.at[pl.ds(3, 3), up[1]], send_z.at[3], recv_z.at[3], down)
    to_side.append(begin(xd.at[:, up[1]], xd.at[:, up[1]], send_s.at[2], recv_s.at[2], sibling))

    project(0, lambda cols: x[:, cols])

    relay_up.wait_recv()
    relay_down.wait_recv()
    to_side.append(begin(xd.at[:, across], xd.at[:, across], send_s.at[3], recv_s.at[3], sibling))
    for copy in far_copies:
        copy.wait_recv()
    for m in range(6):
        for j in range(8):
            first = SLOTS + m * 128 + j * 16
            val[first : first + 16, :] = jnp.where(far[j] > m * RATE, 1.0, 0.0)
    bias[...] = jnp.where(val[...] > 0.5, 0.0, MASKED).astype(BF16)
    for copy in to_side:
        copy.wait_recv()

    project(SLOTS, lambda cols: xd[:, :, :, cols].reshape(SLOTS, WIDTH if isinstance(cols, slice) else BLOCK))

    for copy in to_side + far_copies + near_copies + x_copies + [to_up, to_down, relay_up, relay_down]:
        copy.wait_send()

    def close_keys(pair, a, third):
        rows = slice(third * PART, third * PART + PART)
        mine = lax.broadcasted_iota(jnp.int32, (PART, 128), 1) // 64 == a
        slot = lax.rem(pair // 2, 2)
        for offset, left, right in ((0, grad[a], q_cat[a]), (BLOCK, prob[a], do_cat[a])):
            lanes = pl.ds(pl.multiple_of(lax.rem(pair, 2) * 128 + offset, 128), 128)
            part = dot(left[rows, :], right[...]).astype(BF16)
            dkv[slot, rows, lanes] = jnp.where(mine, part, dkv[slot, rows, lanes])

    own_half = pl.multiple_of(core * 384, 384)
    its_half = pl.multiple_of((1 - core) * 384, 384)

    def parity(r):
        return r % 2 if isinstance(r, int) else lax.rem(r, 2)

    def axis_copies(r, t, axis, source, landing, send, recv, height):
        copies = []
        for d in (2, 1, 3):
            moved = dict(at)
            moved[axis] = lax.rem(at[axis] + d, SIDE)
            device = (moved["y"] * SIDE + moved["x"], moved["z"] * 2 + core)
            if height:
                src = source.at[r, t, pl.ds(pl.multiple_of(moved[axis] * height, height), height), :]
            else:
                src = source.at[r, t, moved[axis]]
            copies.append(remote(src, landing.at[r, t, d - 1], send.at[r, t, d - 1], recv.at[r, t, d - 1], device))
        return copies

    def pair_copy(r, t):
        src = g.at[parity(r), t, pl.ds(its_half, 384), :]
        return remote(src, half.at[r, t], send0.at[r, t], recv0.at[r, t], sibling)

    def a_copies(r, t):
        return axis_copies(r, t, ORDERS[t][0], pair_sum, from_a, send_a, recv_a, 96)

    def b_copies(r, t):
        return axis_copies(r, t, ORDERS[t][1], owned, from_b, send_b, recv_b, 24)

    def c_copies(r, t):
        return axis_copies(r, t, ORDERS[t][2], spread, from_c, send_c, recv_c, 0)

    def stage_pair(r, parts):
        for t in range(3):
            g[parity(r), t] = dot(perm[t], parts(t).astype(BF16)).astype(BF16)
            pair_copy(r, t).start()

    def stage_qkv(r):
        slot = parity(r)

        def parts(t):
            if t == 0:
                return dot(x_t[:, :SLOTS], dq_round[slot])
            return dot(x_t[...], dkv[slot, :, (t - 1) * BLOCK : t * BLOCK])

        stage_pair(r, parts)

    def stage_a(r):
        for t in range(3):
            copy = pair_copy(r, t)
            copy.wait_recv()
            mine = g[parity(r), t, pl.ds(own_half, 384), :].astype(F32)
            pair_sum[r, t] = (mine + half[r, t].astype(F32)).astype(BF16)
            for copy in a_copies(r, t):
                copy.start()

    def stage_b(r):
        for t in range(3):
            mine = pl.multiple_of(at[ORDERS[t][0]] * 96, 96)
            total = g[parity(r), t, pl.ds(pl.multiple_of(own_half + mine, 96), 96), :].astype(F32)
            total = total + half[r, t, pl.ds(mine, 96), :].astype(F32)
            for copy in a_copies(r, t):
                copy.wait_recv()
            for d in range(3):
                total = total + from_a[r, t, d].astype(F32)
            owned[r, t] = total
            for copy in b_copies(r, t):
                copy.start()

    def stage_c(r):
        for t in range(3):
            total = owned[r, t, pl.ds(pl.multiple_of(at[ORDERS[t][1]] * 24, 24), 24), :]
            for copy in b_copies(r, t):
                copy.wait_recv()
            for d in range(3):
                total = total + from_b[r, t, d]
            for c in range(SIDE):
                spread[r, t, c, :6, :] = total[c * 6 : c * 6 + 6]
                spread[r, t, c, 6:, :] = jnp.zeros((2, BLOCK), F32)
            for copy in c_copies(r, t):
                copy.start()

    def stage_out(r):
        for t in range(3):
            total = spread[r, t, at[ORDERS[t][2]]]
            for copy in c_copies(r, t):
                copy.wait_recv()
            for d in range(3):
                total = total + from_c[r, t, d]
            total = total[:6] * factor
            if r < 3:
                first = t * WIDTH + r * BLOCK
                oq_ref[:, first : first + BLOCK] = total
            else:
                oo_ref[:, t * BLOCK : t * BLOCK + BLOCK] = total

    def sent(r):
        for t in range(3):
            for copy in a_copies(r, t) + b_copies(r, t) + c_copies(r, t):
                copy.wait_send()

    @pl.loop(0, HEADS // 2)
    def _(pair):
        lanes = pl.ds(pl.multiple_of(pair * 128, 128), 128)
        before = lax.max(pair - 1, 0)
        done = lax.max(pair // 2 - 1, 0)
        lane = lax.broadcasted_iota(jnp.int32, (KEYS, 128), 1)
        lane_q = lax.broadcasted_iota(jnp.int32, (SLOTS, 128), 1)
        nothing = jnp.zeros((SLOTS, 128), BF16)

        def head_rows(a):
            return pl.ds(pl.multiple_of(pair * 128 + a * 64, 64), 64)

        def open_head(a):
            own = slice(a * 64, a * 64 + 64)
            keys[a][...] = jnp.where(lane // 64 == a, k_tok[:, lanes], bias[...])
            q_rows[a][own, :] = q_t[head_rows(a), :]
            do_rows[a][own, :] = do_t[head_rows(a), :]

        def score_part(step, part):
            a, block = step // 3, step % 3
            rows = slice(part * PART, part * PART + PART)
            cols = slice(block * BLOCK, block * BLOCK + BLOCK)
            s = dot(keys[a][rows, :], q_rows[a][:, cols])
            scores[step % 2][rows, :] = s
            return jnp.max(s, axis=0, keepdims=True)

        def top(parts):
            return jnp.maximum(jnp.maximum(parts[0], parts[1]), parts[2])

        open_head(0)
        peak = top([score_part(0, part) for part in range(3)])
        open_head(1)
        for step in range(6):
            a, block = step // 3, step % 3
            cols = slice(block * BLOCK, block * BLOCK + BLOCK)
            score = scores[step % 2]
            peaks, sums = [], []
            for part in range(3):
                rows = slice(part * PART, part * PART + PART)
                if step < 5:
                    peaks.append(score_part(step + 1, part))
                raw = jnp.exp(score[rows, :] - peak)
                score[rows, :] = raw
                sums.append(jnp.sum(raw, axis=0, keepdims=True))
            inverse = 1.0 / (sums[0] + sums[1] + sums[2])
            for part in range(3):
                rows = slice(part * PART, part * PART + PART)
                grad_p[rows, :] = dot(v_tok[rows, lanes], do_rows[a][:, cols])
                prob[a][rows, cols] = (score[rows, :] * inverse).astype(BF16)
            out = dot(v_t[head_rows(a), :], prob[a][:, cols]).astype(BF16)
            o_t[head_rows(a), cols] = out
            if a == 0:
                close_keys(before, 1, block)
            else:
                close_keys(pair, 0, block)
            delta = jnp.sum(do_t[head_rows(a), cols].astype(F32) * out.astype(F32), axis=0, keepdims=True)
            for part in range(3):
                rows = slice(part * PART, part * PART + PART)
                grad[a][rows, cols] = (score[rows, :] * ((grad_p[rows, :] - delta) * inverse)).astype(BF16)
            dq_t[a * 64 : a * 64 + 64, cols] = (dot(k_t[head_rows(a), :], grad[a][:, cols]) * 0.125).astype(BF16)
            if step < 5:
                peak = top(peaks)
            if step == 2:
                @pl.when((pair == 2) | (pair == 4))
                def _():
                    stage_qkv(done)

                @pl.when((pair == 3) | (pair == 5))
                def _():
                    stage_b(done)

                @pl.when(pair == 4)
                def _():
                    stage_out(0)

            if block == 2:
                half_lanes = lane_q // 64 == a
                q_cat[a][...] = jnp.where(half_lanes, q_tok[:, lanes], nothing)
                do_cat[a][...] = jnp.where(half_lanes, do_tok[:, lanes], nothing)
        dq_round[lax.rem(pair // 2, 2), :, pl.ds(pl.multiple_of(lax.rem(pair, 2) * 128, 128), 128)] = dq_t[...].T

        @pl.when((pair == 2) | (pair == 4))
        def _():
            stage_a(done)

        @pl.when((pair == 3) | (pair == 5))
        def _():
            stage_c(done)

    for third in range(3):
        close_keys(HEADS // 2 - 1, 1, third)
    for t in range(3):
        pair_copy(0, t).wait_send()
    stage_qkv(2)
    for t in range(3):
        pair_copy(1, t).wait_send()
    stage_pair(3, lambda t: dot(o_t[...], mg[:, t * BLOCK : t * BLOCK + BLOCK]))
    stage_a(2)
    do_tok[...] = o_t[...].T
    stage_a(3)

    @pl.loop(0, 3)
    def _(c):
        cols = pl.ds(pl.multiple_of(c * BLOCK, BLOCK), BLOCK)
        mixed = x[:, cols].astype(F32) + dot(do_tok[...], wout[:, cols])
        q_tok[:, cols] = (mixed * val[:SLOTS, :1]).astype(BF16)

    store = pltpu.make_async_copy(q_tok, att_ref, load.at[0])
    store.start()
    stage_out(1)
    for stage in (stage_b, stage_c, stage_out):
        stage(2)
        stage(3)
    for r in range(4):
        sent(r)
    for r in (2, 3):
        for t in range(3):
            pair_copy(r, t).wait_send()
    store.wait()


def whole(feats, gain, w_embed, target, cot, w_qkv, w_out, factor):
    tall, wide, square = (KEYS, WIDTH), (WIDTH, KEYS), (SLOTS, WIDTH)
    vmem, anywhere = pl.BlockSpec(memory_space=pltpu.VMEM), pl.BlockSpec(memory_space=pl.ANY)
    dma = pltpu.SemaphoreType.DMA
    half16 = lambda *shapes: [pltpu.VMEM(shape, BF16) for shape in shapes]
    full32 = lambda *shapes: [pltpu.VMEM(shape, F32) for shape in shapes]
    scratch = half16(square, (6, 8, 16, WIDTH)) + full32((KEYS, 128)) + half16((KEYS, 128))
    scratch += half16(square, tall, tall, square, square, wide, wide, square, wide, square, square, square)
    scratch += half16((128, SLOTS), (2, SLOTS, BLOCK), (2, KEYS, 2 * BLOCK))
    scratch += full32((KEYS, BLOCK), (KEYS, BLOCK), (KEYS, BLOCK)) + half16(tall, tall, tall, tall)
    scratch += half16(*[(KEYS, 128)] * 2, *[(128, SLOTS)] * 4, *[(SLOTS, 128)] * 4, (3, WIDTH, WIDTH))
    scratch += full32((16, 8, 128), (16, 8, 128), (16, 128), (8, 16, 128)) + half16((6, 16, WIDTH))
    scratch += half16((2, 3, WIDTH, BLOCK), (4, 3, 384, BLOCK), (4, 3, 384, BLOCK), (4, 3, 3, 96, BLOCK))
    scratch += full32((4, 3, 96, BLOCK), (4, 3, 3, 24, BLOCK), (4, 3, SIDE, 8, BLOCK), (4, 3, 3, 8, BLOCK))
    scratch += [dma((8,)), dma((2, 15)), dma((2, 15)), dma((15,)), dma((15,)), dma((7,)), dma((7,))]
    scratch += [dma((4,))] * 4 + [dma((4, 3))] * 2 + [dma((4, 3, 3))] * 6
    return pl.pallas_call(
        functools.partial(whole_kernel, factor),
        out_shape=(
            jax.ShapeDtypeStruct(square, BF16),
            jax.ShapeDtypeStruct((6, 3 * WIDTH), F32),
            jax.ShapeDtypeStruct((6, WIDTH), F32),
        ),
        in_specs=[anywhere, vmem, anywhere, vmem, anywhere, anywhere, anywhere, vmem],
        out_specs=(anywhere, vmem, vmem),
        scratch_shapes=scratch,
        compiler_params=pltpu.CompilerParams(
            collective_id=1, has_side_effects=True, vmem_limit_bytes=63 * 1024 * 1024
        ),
        cost_estimate=pl.CostEstimate(flops=30_000_000_000, bytes_accessed=16_000_000, transcendentals=14_000_000),
        name="whole",
    )(feats, gain, w_embed, target, cot, w_qkv, w_out, jnp.asarray(row_orders()))


def shards(tile_feats, norm_gain, w_embed, slide_of_tile, w_qkv, w_out, cotangent):
    factor = (lax.axis_size("slide") * lax.axis_size("seq") * SLOTS) ** (-0.5)
    output, grad_qkv, grad_out = whole(
        tile_feats, norm_gain.reshape(1, WIDE), w_embed, slide_of_tile.reshape(1, TILES),
        cotangent[0], w_qkv, w_out, factor,
    )
    return (output[None], grad_qkv, grad_out)


def solution(mesh):
    return jax.shard_map(
        shards,
        mesh=mesh,
        in_specs=(
            P(("slide", "seq"), None),
            P(),
            P(),
            P(("slide", "seq"), None),
            P(),
            P(),
            P("slide", "seq", None),
        ),
        out_specs=(P("slide", "seq", None), P(("slide", "seq"), None), P(("slide", "seq"), None)),
        check_vma=False,
    )
```

time: 1090 us -> 142 us (0.13); the launches traced: 1080 us -> 142 us
  blocking collectives: 403 us -> 0 us
  local copies, waits for them, and re-layouts: 204 us -> 4.93 us
  starting transfers between devices: 178 us -> 0 us
  matrix products: 175 us -> 0 us
  Pallas kernels: 0 us -> 136 us
  other arithmetic: 78.9 us -> 0 us
  waiting for transfers between devices: 22.3 us -> 0 us
  between operations: 16 us -> 0.66 us
    unnamed x2 -> x0, blocking collectives: 378 us -> none
    dot_general x80 -> x0, matrix products: 175 us -> none  [the longest x12 47.7 us: head_pass(): jnp.dot(prob_bf16, values_all, preferred_element_type=jnp.float32)]
    unnamed x65 -> x0, starting transfers between devices: 174 us -> none
    pallas_call x0 -> x1, Pallas kernels: none -> 136 us  [whole(): pl.pallas_call(functools.partial(whole_kernel, factor), out_shape=(jax.Sh...]
    unnamed x77 -> x7, local copies, waits for them, and re-layouts: 119 us -> 3.64 us
    dynamic_slice x96 -> x0, local copies, waits for them, and re-layouts: 51.1 us -> none  [block_pass(): lax.map(lambda group: head_pass(*group, key_mask), (to_heads(qkv[:, :widt...]
    div x13 -> x0, other arithmetic: 38.1 us -> none  [the longest x12 38.1 us: head_pass(): prob_exact = raw_weights / jnp.sum(raw_weights, axis=-1, keepdims=True)]
    reduce_sum x27 -> x0, other arithmetic: 27.8 us -> none  [the longest x12 12.4 us: head_pass(): prob_exact = raw_weights / jnp.sum(raw_weights, axis=-1, keepdims=True)]
  transfers between devices with their start and end apart: 67 -> 0, of which waited for: 2 -> 0; matrix products, arithmetic and copies ran while one was open for 7% -> 0% of each run, Pallas kernels for 0% -> 0%
where the time goes in v3:
time: 142 us
  Pallas kernels  136 us (96%)
  local copies, waits for them, and re-layouts  4.93 us (3%)
    pallas_call x1, Pallas kernels, whole(): pl.pallas_call(functools.partial(whole_kernel, factor), out_shape=(jax.Sh...  136 us
    unnamed x7, local copies, waits for them, and re-layouts  3.64 us

profile of v3, /device:TPU:1, one launch (start us, length us, event | category | flops | bytes accessed | tf_op | source)
XLA Modules:
  0.0 141.9 jit_solution(16410718171700482058)
XLA Ops:
  0.6 1.3 reshape.12.gain_ref
  1.9 136.3 %whole.1 = (bf16[768,768]{1,0:T(8,128)(2,1)}, f32[6,2304]{1,0:T(8,128)}, f32[6,768]{1,0:T(8,128)}) custom-call(bf16[384,1536]{1,0:T(8,128)(2,1)} %feats_ref.1, f32[1,1536]{1,0:T(1,128)} %reshape.12.gain_ref, bf16[1536,768]{1,0:T(8,128)(2,1)} %we_ref.1, s32[1,384]{1,0:T(1,128)} %bitcast.5, bf16[768,768]{1,0:T(8,128)(2,1)} %bitcast.4, ...), custom_call_target="tpu_custom_call" | custom-call | flops 30000001024 | bytes 16000000 | tf_op jit(solution)/shard_map/whole/pallas_call | solution.py:480
  138.2 0.0 copy-start
  138.2 0.0 copy-start.1
  138.2 2.4 %copy.14 = bf16[1,768,768]{2,1,0:T(8,128)(2,1)} copy(bf16[1,768,768]{2,1,0:T(8,128)(2,1)} %bitcast.3) | data formatting | bytes 2359296
  140.6 0.0 copy-done
  140.6 0.6 copy.15
  141.3 0.0 copy-done.1
  141.3 0.6 copy.16
Async XLA Ops:
  138.2 2.4 %copy-start = (f32[6,2304]{1,0:T(8,128)S(1)}, f32[6,2304]{1,0:T(8,128)}, u32[]{:S(2)}) copy-start(f32[6,2304]{1,0:T(8,128)} %get-tuple-element.13) | copy-start | bytes 165892
  138.2 3.0 %copy-start.1 = (f32[6,768]{1,0:T(8,128)S(1)}, f32[6,768]{1,0:T(8,128)}, u32[]{:S(2)}) copy-start(f32[6,768]{1,0:T(8,128)} %get-tuple-element.14) | copy-start | bytes 55300

commit v4 on v3

--- a/solution.py
+++ b/solution.py
@@ -116,8 +116,8 @@
         moved = [v - center for v in values]
         spread_sq = sum(jnp.sum(v * v, axis=-1, keepdims=True) for v in moved) * (1.0 / WIDE)
         scale = lax.rsqrt(spread_sq + 1e-06)
-        normed[low, :] = (moved[0] * scale * gain_ref[:, :WIDTH]).astype(BF16)
-        normed[high, :] = (moved[1] * scale * gain_ref[:, WIDTH:]).astype(BF16)
+        normed[low, :] = (moved[0] * scale * gain_ref[:WIDTH].reshape(1, WIDTH)).astype(BF16)
+        normed[high, :] = (moved[1] * scale * gain_ref[WIDTH:].reshape(1, WIDTH)).astype(BF16)
 
     pl.semaphore_wait(barrier, 22)
     near_copies = [
@@ -230,14 +230,13 @@
     for copy in to_side + far_copies + near_copies + x_copies + [to_up, to_down, relay_up, relay_down]:
         copy.wait_send()
 
-    def close_keys(pair, a, third):
-        rows = slice(third * PART, third * PART + PART)
-        mine = lax.broadcasted_iota(jnp.int32, (PART, 128), 1) // 64 == a
+    def close_keys(pair, a, which):
+        mine = lax.broadcasted_iota(jnp.int32, (KEYS, 128), 1) // 64 == a
         slot = lax.rem(pair // 2, 2)
-        for offset, left, right in ((0, grad[a], q_cat[a]), (BLOCK, prob[a], do_cat[a])):
-            lanes = pl.ds(pl.multiple_of(lax.rem(pair, 2) * 128 + offset, 128), 128)
-            part = dot(left[rows, :], right[...]).astype(BF16)
-            dkv[slot, rows, lanes] = jnp.where(mine, part, dkv[slot, rows, lanes])
+        left, right, offset = ((prob[a], do_cat[a], BLOCK), (grad[a], q_cat[a], 0))[which]
+        lanes = pl.ds(pl.multiple_of(lax.rem(pair, 2) * 128 + offset, 128), 128)
+        part = dot(left[...], right[...]).astype(BF16)
+        dkv[slot, :, lanes] = jnp.where(mine, part, dkv[slot, :, lanes])
 
     own_half = pl.multiple_of(core * 384, 384)
     its_half = pl.multiple_of((1 - core) * 384, 384)
@@ -358,50 +357,43 @@
             q_rows[a][own, :] = q_t[head_rows(a), :]
             do_rows[a][own, :] = do_t[head_rows(a), :]
 
-        def score_part(step, part):
+        def score_step(step):
             a, block = step // 3, step % 3
-            rows = slice(part * PART, part * PART + PART)
-            cols = slice(block * BLOCK, block * BLOCK + BLOCK)
-            s = dot(keys[a][rows, :], q_rows[a][:, cols])
-            scores[step % 2][rows, :] = s
+            s = dot(keys[a][...], q_rows[a][:, block * BLOCK : block * BLOCK + BLOCK])
+            scores[step % 2][...] = s
             return jnp.max(s, axis=0, keepdims=True)
 
-        def top(parts):
-            return jnp.maximum(jnp.maximum(parts[0], parts[1]), parts[2])
-
         open_head(0)
-        peak = top([score_part(0, part) for part in range(3)])
+        peak = score_step(0)
         open_head(1)
         for step in range(6):
             a, block = step // 3, step % 3
             cols = slice(block * BLOCK, block * BLOCK + BLOCK)
             score = scores[step % 2]
-            peaks, sums = [], []
+            sums = []
+            if step < 5:
+                next_peak = score_step(step + 1)
             for part in range(3):
                 rows = slice(part * PART, part * PART + PART)
-                if step < 5:
-                    peaks.append(score_part(step + 1, part))
                 raw = jnp.exp(score[rows, :] - peak)
                 score[rows, :] = raw
                 sums.append(jnp.sum(raw, axis=0, keepdims=True))
             inverse = 1.0 / (sums[0] + sums[1] + sums[2])
+            grad_p[...] = dot(v_tok[:, lanes], do_rows[a][:, cols])
             for part in range(3):
                 rows = slice(part * PART, part * PART + PART)
-                grad_p[rows, :] = dot(v_tok[rows, lanes], do_rows[a][:, cols])
                 prob[a][rows, cols] = (score[rows, :] * inverse).astype(BF16)
             out = dot(v_t[head_rows(a), :], prob[a][:, cols]).astype(BF16)
             o_t[head_rows(a), cols] = out
-            if a == 0:
-                close_keys(before, 1, block)
-            else:
-                close_keys(pair, 0, block)
+            if block < 2:
+                close_keys(before if a == 0 else pair, 1 - a, block)
             delta = jnp.sum(do_t[head_rows(a), cols].astype(F32) * out.astype(F32), axis=0, keepdims=True)
             for part in range(3):
                 rows = slice(part * PART, part * PART + PART)
                 grad[a][rows, cols] = (score[rows, :] * ((grad_p[rows, :] - delta) * inverse)).astype(BF16)
             dq_t[a * 64 : a * 64 + 64, cols] = (dot(k_t[head_rows(a), :], grad[a][:, cols]) * 0.125).astype(BF16)
             if step < 5:
-                peak = top(peaks)
+                peak = next_peak
             if step == 2:
                 @pl.when((pair == 2) | (pair == 4))
                 def _():
@@ -429,8 +421,8 @@
         def _():
             stage_c(done)
 
-    for third in range(3):
-        close_keys(HEADS // 2 - 1, 1, third)
+    for which in range(2):
+        close_keys(HEADS // 2 - 1, 1, which)
     for t in range(3):
         pair_copy(0, t).wait_send()
     stage_qkv(2)
@@ -498,7 +490,7 @@
 def shards(tile_feats, norm_gain, w_embed, slide_of_tile, w_qkv, w_out, cotangent):
     factor = (lax.axis_size("slide") * lax.axis_size("seq") * SLOTS) ** (-0.5)
     output, grad_qkv, grad_out = whole(
-        tile_feats, norm_gain.reshape(1, WIDE), w_embed, slide_of_tile.reshape(1, TILES),
+        tile_feats, norm_gain, w_embed, slide_of_tile.reshape(1, TILES),
         cotangent[0], w_qkv, w_out, factor,
     )
     return (output[None], grad_qkv, grad_out)

time: 142 us -> 149 us (1.049)
  Pallas kernels: 136 us -> 145 us
    pallas_call x1, Pallas kernels: 136 us -> 145 us  [whole(): pl.pallas_call(functools.partial(whole_kernel, factor), out_shape=(jax.Sh...]
where the time goes in v4:
time: 149 us
  Pallas kernels  145 us (97%)
  local copies, waits for them, and re-layouts  3.64 us (2%)
    pallas_call x1, Pallas kernels, whole(): pl.pallas_call(functools.partial(whole_kernel, factor), out_shape=(jax.Sh...  145 us
    unnamed x7, local copies, waits for them, and re-layouts  3.64 us

profile of v4, /device:TPU:1, one launch (start us, length us, event | category | flops | bytes accessed | tf_op | source)
XLA Modules:
  0.0 149.1 jit_solution(11825553840726847412)
XLA Ops:
  0.6 144.8 %whole.1 = (bf16[768,768]{1,0:T(8,128)(2,1)}, f32[6,2304]{1,0:T(8,128)}, f32[6,768]{1,0:T(8,128)}) custom-call(bf16[384,1536]{1,0:T(8,128)(2,1)} %feats_ref.1, f32[1536]{0:T(1024)} %gain_ref.1, bf16[1536,768]{1,0:T(8,128)(2,1)} %we_ref.1, s32[1,384]{1,0:T(1,128)} %bitcast.5, bf16[768,768]{1,0:T(8,128)(2,1)} %bitcast.4, bf16[768,2304]{1,0:T(8,128)(2,1)} %wqkv_ref.1, ...), custom_call_target="tpu_custom_call" | custom-call | flops 30000001024 | bytes 16000000 | tf_op jit(solution)/shard_map/whole/pallas_call | solution.py:472
  145.4 0.0 copy-start
  145.4 0.0 copy-start.1
  145.4 2.4 %copy.14 = bf16[1,768,768]{2,1,0:T(8,128)(2,1)} copy(bf16[1,768,768]{2,1,0:T(8,128)(2,1)} %bitcast.3) | data formatting | bytes 2359296
  147.8 0.0 copy-done
  147.8 0.6 copy.15
  148.5 0.0 copy-done.1
  148.5 0.6 copy.16
Async XLA Ops:
  145.4 2.4 %copy-start = (f32[6,2304]{1,0:T(8,128)S(1)}, f32[6,2304]{1,0:T(8,128)}, u32[]{:S(2)}) copy-start(f32[6,2304]{1,0:T(8,128)} %get-tuple-element.13) | copy-start | bytes 165892
  145.4 3.0 %copy-start.1 = (f32[6,768]{1,0:T(8,128)S(1)}, f32[6,768]{1,0:T(8,128)}, u32[]{:S(2)}) copy-start(f32[6,768]{1,0:T(8,128)} %get-tuple-element.14) | copy-start | bytes 55300

commit v5 on v3

--- a/solution.py
+++ b/solution.py
@@ -18,6 +18,8 @@
 KEYS = 1536
 BLOCK = 256
 PART = 512
+CHAIN = 64
+PARTS = KEYS // PART
 SIDE = 4
 MASKED = -1e30
 BF16 = jnp.bfloat16
@@ -116,8 +118,8 @@
         moved = [v - center for v in values]
         spread_sq = sum(jnp.sum(v * v, axis=-1, keepdims=True) for v in moved) * (1.0 / WIDE)
         scale = lax.rsqrt(spread_sq + 1e-06)
-        normed[low, :] = (moved[0] * scale * gain_ref[:, :WIDTH]).astype(BF16)
-        normed[high, :] = (moved[1] * scale * gain_ref[:, WIDTH:]).astype(BF16)
+        normed[low, :] = (moved[0] * scale * gain_ref[:WIDTH].reshape(1, WIDTH)).astype(BF16)
+        normed[high, :] = (moved[1] * scale * gain_ref[WIDTH:].reshape(1, WIDTH)).astype(BF16)
 
     pl.semaphore_wait(barrier, 22)
     near_copies = [
@@ -361,34 +363,35 @@
         def score_part(step, part):
             a, block = step // 3, step % 3
             rows = slice(part * PART, part * PART + PART)
-            cols = slice(block * BLOCK, block * BLOCK + BLOCK)
-            s = dot(keys[a][rows, :], q_rows[a][:, cols])
+            s = dot(keys[a][rows, :], q_rows[a][:, block * BLOCK : block * BLOCK + BLOCK])
             scores[step % 2][rows, :] = s
             return jnp.max(s, axis=0, keepdims=True)
 
-        def top(parts):
-            return jnp.maximum(jnp.maximum(parts[0], parts[1]), parts[2])
+        def short(part):
+            return [slice(first, first + CHAIN) for first in range(part * PART, part * PART + PART, CHAIN)]
 
         open_head(0)
-        peak = top([score_part(0, part) for part in range(3)])
+        peaks = [score_part(0, part) for part in range(PARTS)]
         open_head(1)
         for step in range(6):
             a, block = step // 3, step % 3
             cols = slice(block * BLOCK, block * BLOCK + BLOCK)
             score = scores[step % 2]
-            peaks, sums = [], []
-            for part in range(3):
-                rows = slice(part * PART, part * PART + PART)
+            peak = functools.reduce(jnp.maximum, peaks)
+            peaks, total = [], jnp.zeros((8, BLOCK), F32)
+            for part in range(PARTS):
                 if step < 5:
                     peaks.append(score_part(step + 1, part))
-                raw = jnp.exp(score[rows, :] - peak)
-                score[rows, :] = raw
-                sums.append(jnp.sum(raw, axis=0, keepdims=True))
-            inverse = 1.0 / (sums[0] + sums[1] + sums[2])
-            for part in range(3):
-                rows = slice(part * PART, part * PART + PART)
-                grad_p[rows, :] = dot(v_tok[rows, lanes], do_rows[a][:, cols])
-                prob[a][rows, cols] = (score[rows, :] * inverse).astype(BF16)
+                for rows in short(part):
+                    raw = jnp.exp(score[rows, :] - peak)
+                    score[rows, :] = raw
+                    total = total + jnp.sum(raw.reshape(CHAIN // 8, 8, BLOCK), axis=0)
+            inverse = 1.0 / jnp.sum(total, axis=0, keepdims=True)
+            for part in range(PARTS):
+                whole_part = slice(part * PART, part * PART + PART)
+                grad_p[whole_part, :] = dot(v_tok[whole_part, lanes], do_rows[a][:, cols])
+                for rows in short(part):
+                    prob[a][rows, cols] = (score[rows, :] * inverse).astype(BF16)
             out = dot(v_t[head_rows(a), :], prob[a][:, cols]).astype(BF16)
             o_t[head_rows(a), cols] = out
             if a == 0:
@@ -396,12 +399,10 @@
             else:
                 close_keys(pair, 0, block)
             delta = jnp.sum(do_t[head_rows(a), cols].astype(F32) * out.astype(F32), axis=0, keepdims=True)
-            for part in range(3):
-                rows = slice(part * PART, part * PART + PART)
-                grad[a][rows, cols] = (score[rows, :] * ((grad_p[rows, :] - delta) * inverse)).astype(BF16)
+            for part in range(PARTS):
+                for rows in short(part):
+                    grad[a][rows, cols] = (score[rows, :] * ((grad_p[rows, :] - delta) * inverse)).astype(BF16)
             dq_t[a * 64 : a * 64 + 64, cols] = (dot(k_t[head_rows(a), :], grad[a][:, cols]) * 0.125).astype(BF16)
-            if step < 5:
-                peak = top(peaks)
             if step == 2:
                 @pl.when((pair == 2) | (pair == 4))
                 def _():
@@ -495,12 +496,41 @@
     )(feats, gain, w_embed, target, cot, w_qkv, w_out, jnp.asarray(row_orders()))
 
 
+def hand_over_kernel(*refs):
+    ins, outs, held, sem_in, sem_out = refs[:3], refs[3:6], refs[6:9], refs[9], refs[10]
+    pieces = [(0, slice(first, first + 192)) for first in range(0, SLOTS, 192)] + [(1, slice(0, 6)), (2, slice(0, 6))]
+    arriving, leaving = [], []
+    for n, (which, rows) in enumerate(pieces):
+        arriving.append(pltpu.make_async_copy(ins[which].at[rows], held[which].at[rows], sem_in.at[n]))
+        leaving.append(pltpu.make_async_copy(held[which].at[rows], outs[which].at[rows], sem_out.at[n]))
+    for copy in arriving:
+        copy.start()
+    for first, second in zip(arriving, leaving):
+        first.wait()
+        second.start()
+    for copy in leaving:
+        copy.wait()
+
+
+def hand_over(*arrays):
+    anywhere = pl.BlockSpec(memory_space=pl.ANY)
+    return pl.pallas_call(
+        hand_over_kernel,
+        out_shape=tuple(jax.ShapeDtypeStruct(a.shape, a.dtype) for a in arrays),
+        in_specs=[anywhere] * 3,
+        out_specs=(anywhere,) * 3,
+        scratch_shapes=[pltpu.VMEM(a.shape, a.dtype) for a in arrays] + [pltpu.SemaphoreType.DMA((6,))] * 2,
+        compiler_params=pltpu.CompilerParams(vmem_limit_bytes=63 * 1024 * 1024),
+        name="hand_over",
+    )(*arrays)
+
+
 def shards(tile_feats, norm_gain, w_embed, slide_of_tile, w_qkv, w_out, cotangent):
     factor = (lax.axis_size("slide") * lax.axis_size("seq") * SLOTS) ** (-0.5)
-    output, grad_qkv, grad_out = whole(
-        tile_feats, norm_gain.reshape(1, WIDE), w_embed, slide_of_tile.reshape(1, TILES),
+    output, grad_qkv, grad_out = hand_over(*whole(
+        tile_feats, norm_gain, w_embed, slide_of_tile.reshape(1, TILES),
         cotangent[0], w_qkv, w_out, factor,
-    )
+    ))
     return (output[None], grad_qkv, grad_out)
 
 

time: 142 us -> 139 us (0.979)
  local copies, waits for them, and re-layouts: 4.93 us -> 0 us
  Pallas kernels: 136 us -> 138 us
    unnamed x7 -> x0, local copies, waits for them, and re-layouts: 3.64 us -> none
    pallas_call x0 -> x1, Pallas kernels: none -> 2.09 us  [hand_over(): pl.pallas_call(hand_over_kernel, out_shape=tuple((jax.ShapeDtypeStruct(a....]
where the time goes in v5:
time: 139 us; the launch traced here: 138 us
  Pallas kernels  138 us (99%)
    pallas_call x1, Pallas kernels, whole(): pl.pallas_call(functools.partial(whole_kernel, factor), out_shape=(jax.Sh...  136 us

profile of v5, /device:TPU:1, one launch (start us, length us, event | category | flops | bytes accessed | tf_op | source)
XLA Modules:
  0.0 138.5 jit_solution(12943496730762413447)
XLA Ops:
  0.6 135.6 %whole.1 = (bf16[768,768]{1,0:T(8,128)(2,1)}, f32[6,2304]{1,0:T(8,128)}, f32[6,768]{1,0:T(8,128)}) custom-call(bf16[384,1536]{1,0:T(8,128)(2,1)} %feats_ref.1, f32[1536]{0:T(1024)} %gain_ref.1, bf16[1536,768]{1,0:T(8,128)(2,1)} %we_ref.1, s32[1,384]{1,0:T(1,128)} %bitcast.5, bf16[768,768]{1,0:T(8,128)(2,1)} %bitcast.3, bf16[768,2304]{1,0:T(8,128)(2,1)} %wqkv_ref.1, ...), custom_call_target="tpu_custom_call" | custom-call | flops 30000001024 | bytes 16000000 | tf_op jit(solution)/shard_map/whole/pallas_call | solution.py:481
  136.2 2.1 %hand_over.1 = (bf16[768,768]{1,0:T(8,128)(2,1)}, f32[6,2304]{1,0:T(8,128)}, f32[6,768]{1,0:T(8,128)}) custom-call(bf16[768,768]{1,0:T(8,128)(2,1)} %get-tuple-element.9.refs_0_, f32[6,2304]{1,0:T(8,128)} %get-tuple-element.10.refs_1_, f32[6,768]{1,0:T(8,128)} %get-tuple-element.11.refs_2_), custom_call_target="tpu_custom_call" | custom-call | tf_op jit(solution)/shard_map/hand_over/pallas_call | solution.py:517

commit v6 on v5

--- a/solution.py
+++ b/solution.py
@@ -232,14 +232,14 @@
     for copy in to_side + far_copies + near_copies + x_copies + [to_up, to_down, relay_up, relay_down]:
         copy.wait_send()
 
-    def close_keys(pair, a, third):
+    def close_keys(pair, a, which, third):
         rows = slice(third * PART, third * PART + PART)
         mine = lax.broadcasted_iota(jnp.int32, (PART, 128), 1) // 64 == a
         slot = lax.rem(pair // 2, 2)
-        for offset, left, right in ((0, grad[a], q_cat[a]), (BLOCK, prob[a], do_cat[a])):
-            lanes = pl.ds(pl.multiple_of(lax.rem(pair, 2) * 128 + offset, 128), 128)
-            part = dot(left[rows, :], right[...]).astype(BF16)
-            dkv[slot, rows, lanes] = jnp.where(mine, part, dkv[slot, rows, lanes])
+        left, right, offset = ((prob[a], do_cat[a], BLOCK), (grad[a], q_cat[a], 0))[which]
+        lanes = pl.ds(pl.multiple_of(lax.rem(pair, 2) * 128 + offset, 128), 128)
+        part = dot(left[rows, :], right[...]).astype(BF16)
+        dkv[slot, rows, lanes] = jnp.where(mine, part, dkv[slot, rows, lanes])
 
     own_half = pl.multiple_of(core * 384, 384)
     its_half = pl.multiple_of((1 - core) * 384, 384)
@@ -377,6 +377,7 @@
             a, block = step // 3, step % 3
             cols = slice(block * BLOCK, block * BLOCK + BLOCK)
             score = scores[step % 2]
+            closing = (before if a == 0 else pair, 1 - a)
             peak = functools.reduce(jnp.maximum, peaks)
             peaks, total = [], jnp.zeros((8, BLOCK), F32)
             for part in range(PARTS):
@@ -386,23 +387,28 @@
                     raw = jnp.exp(score[rows, :] - peak)
                     score[rows, :] = raw
                     total = total + jnp.sum(raw.reshape(CHAIN // 8, 8, BLOCK), axis=0)
+                if part == 1:
+                    close_keys(*closing, 0, block)
             inverse = 1.0 / jnp.sum(total, axis=0, keepdims=True)
+            out = 0.0
             for part in range(PARTS):
-                whole_part = slice(part * PART, part * PART + PART)
-                grad_p[whole_part, :] = dot(v_tok[whole_part, lanes], do_rows[a][:, cols])
+                keys_of = slice(part * PART, part * PART + PART)
                 for rows in short(part):
                     prob[a][rows, cols] = (score[rows, :] * inverse).astype(BF16)
-            out = dot(v_t[head_rows(a), :], prob[a][:, cols]).astype(BF16)
+                grad_p[keys_of, :] = dot(v_tok[keys_of, lanes], do_rows[a][:, cols])
+                out = out + dot(v_t[head_rows(a), keys_of], prob[a][keys_of, cols])
+            out = out.astype(BF16)
             o_t[head_rows(a), cols] = out
-            if a == 0:
-                close_keys(before, 1, block)
-            else:
-                close_keys(pair, 0, block)
             delta = jnp.sum(do_t[head_rows(a), cols].astype(F32) * out.astype(F32), axis=0, keepdims=True)
+            d_query = 0.0
             for part in range(PARTS):
+                keys_of = slice(part * PART, part * PART + PART)
                 for rows in short(part):
                     grad[a][rows, cols] = (score[rows, :] * ((grad_p[rows, :] - delta) * inverse)).astype(BF16)
-            dq_t[a * 64 : a * 64 + 64, cols] = (dot(k_t[head_rows(a), :], grad[a][:, cols]) * 0.125).astype(BF16)
+                if part == 1:
+                    close_keys(*closing, 1, block)
+                d_query = d_query + dot(k_t[head_rows(a), keys_of], grad[a][keys_of, cols])
+            dq_t[a * 64 : a * 64 + 64, cols] = (d_query * 0.125).astype(BF16)
             if step == 2:
                 @pl.when((pair == 2) | (pair == 4))
                 def _():
@@ -431,7 +437,8 @@
             stage_c(done)
 
     for third in range(3):
-        close_keys(HEADS // 2 - 1, 1, third)
+        for which in range(2):
+            close_keys(HEADS // 2 - 1, 1, which, third)
     for t in range(3):
         pair_copy(0, t).wait_send()
     stage_qkv(2)

time: 139 us -> 142 us (1.022)
  Pallas kernels: 138 us -> 141 us
    pallas_call x1, Pallas kernels: 136 us -> 139 us  [whole(): pl.pallas_call(functools.partial(whole_kernel, factor), out_shape=(jax.Sh...]
where the time goes in v6:
time: 142 us
  Pallas kernels  141 us (99%)
    pallas_call x1, Pallas kernels, whole(): pl.pallas_call(functools.partial(whole_kernel, factor), out_shape=(jax.Sh...  139 us

profile of v6, /device:TPU:1, one launch (start us, length us, event | category | flops | bytes accessed | tf_op | source)
XLA Modules:
  0.0 141.6 jit_solution(18408427938302507205)
XLA Ops:
  0.6 138.7 %whole.1 = (bf16[768,768]{1,0:T(8,128)(2,1)}, f32[6,2304]{1,0:T(8,128)}, f32[6,768]{1,0:T(8,128)}) custom-call(bf16[384,1536]{1,0:T(8,128)(2,1)} %feats_ref.1, f32[1536]{0:T(1024)} %gain_ref.1, bf16[1536,768]{1,0:T(8,128)(2,1)} %we_ref.1, s32[1,384]{1,0:T(1,128)} %bitcast.5, bf16[768,768]{1,0:T(8,128)(2,1)} %bitcast.3, bf16[768,2304]{1,0:T(8,128)(2,1)} %wqkv_ref.1, ...), custom_call_target="tpu_custom_call" | custom-call | flops 30000001024 | bytes 16000000 | tf_op jit(solution)/shard_map/whole/pallas_call | solution.py:488
  139.3 2.1 %hand_over.1 = (bf16[768,768]{1,0:T(8,128)(2,1)}, f32[6,2304]{1,0:T(8,128)}, f32[6,768]{1,0:T(8,128)}) custom-call(bf16[768,768]{1,0:T(8,128)(2,1)} %get-tuple-element.9.refs_0_, f32[6,2304]{1,0:T(8,128)} %get-tuple-element.10.refs_1_, f32[6,768]{1,0:T(8,128)} %get-tuple-element.11.refs_2_), custom_call_target="tpu_custom_call" | custom-call | tf_op jit(solution)/shard_map/hand_over/pallas_call | solution.py:524

commit v7 on v5

--- a/solution.py
+++ b/solution.py
@@ -27,6 +27,7 @@
 MESH = pl.DeviceIdType.MESH
 ORDERS = (("x", "y", "z"), ("y", "z", "x"), ("z", "x", "y"))
 NT = (((1,), (1,)), ((), ()))
+TN = (((0,), (0,)), ((), ()))
 
 
 def row_orders():
@@ -47,8 +48,8 @@
     factor,
     feats_ref, gain_ref, we_ref, target_ref, cot_ref, wqkv_ref, wout_ref, place_ref,
     att_ref, oq_ref, oo_ref,
-    x, xd, val, bias, q_tok, k_tok, v_tok, do_tok, q_t, k_t, v_t, do_t, x_t, mg, o_t, wout,
-    dq_t, dq_round, dkv, score_0, score_1, grad_p, prob_0, prob_1, grad_0, grad_1,
+    x, xd, val, bias, q_tok, k_tok, v_tok, do_tok, q_t, do_t, x_t, mg, o_t, wout,
+    dq_round, dkv, score_0, score_1, grad_p, prob_0, prob_1, grad_0, grad_1,
     key_0, key_1, q_0, q_1, do_0, do_1, qc_0, qc_1, dc_0, dc_1, perm,
     tally, near_all, near, far, own_far,
     g, half, pair_sum, from_a, owned, from_b, spread, from_c,
@@ -193,10 +194,9 @@
         def _(c):
             cols = pl.ds(pl.multiple_of(c * BLOCK, BLOCK), BLOCK)
             x_t[cols, first : first + SLOTS] = rows_of(cols).T
-            for w, tok, turned in ((w_k, k_tok, k_t), (w_v, v_tok, v_t)):
+            for w, tok in ((w_k, k_tok), (w_v, v_tok)):
                 part = dot(rows_of(slice(None)), w[:, cols]).astype(BF16)
                 tok[first : first + SLOTS, cols] = part
-                turned[cols, first : first + SLOTS] = part.T
 
     @pl.loop(0, 3)
     def _(c):
@@ -350,6 +350,7 @@
         lane = lax.broadcasted_iota(jnp.int32, (KEYS, 128), 1)
         lane_q = lax.broadcasted_iota(jnp.int32, (SLOTS, 128), 1)
         nothing = jnp.zeros((SLOTS, 128), BF16)
+        q_slot, q_lanes = lax.rem(pair // 2, 2), pl.ds(pl.multiple_of(lax.rem(pair, 2) * 128, 128), 128)
 
         def head_rows(a):
             return pl.ds(pl.multiple_of(pair * 128 + a * 64, 64), 64)
@@ -392,7 +393,8 @@
                 grad_p[whole_part, :] = dot(v_tok[whole_part, lanes], do_rows[a][:, cols])
                 for rows in short(part):
                     prob[a][rows, cols] = (score[rows, :] * inverse).astype(BF16)
-            out = dot(v_t[head_rows(a), :], prob[a][:, cols]).astype(BF16)
+            out = lax.dot_general(prob[a][:, cols], v_tok[:, lanes], TN, preferred_element_type=F32).astype(BF16)
+            out = out.T[a * 64 : a * 64 + 64]
             o_t[head_rows(a), cols] = out
             if a == 0:
                 close_keys(before, 1, block)
@@ -402,7 +404,9 @@
             for part in range(PARTS):
                 for rows in short(part):
                     grad[a][rows, cols] = (score[rows, :] * ((grad_p[rows, :] - delta) * inverse)).astype(BF16)
-            dq_t[a * 64 : a * 64 + 64, cols] = (dot(k_t[head_rows(a), :], grad[a][:, cols]) * 0.125).astype(BF16)
+            d_query = lax.dot_general(grad[a][:, cols], k_tok[:, lanes], TN, preferred_element_type=F32) * 0.125
+            d_query = jnp.where(lane_q[:BLOCK] // 64 == a, d_query.astype(BF16), dq_round[q_slot, cols, q_lanes])
+            dq_round[q_slot, cols, q_lanes] = d_query
             if step == 2:
                 @pl.when((pair == 2) | (pair == 4))
                 def _():
@@ -420,8 +424,6 @@
                 half_lanes = lane_q // 64 == a
                 q_cat[a][...] = jnp.where(half_lanes, q_tok[:, lanes], nothing)
                 do_cat[a][...] = jnp.where(half_lanes, do_tok[:, lanes], nothing)
-        dq_round[lax.rem(pair // 2, 2), :, pl.ds(pl.multiple_of(lax.rem(pair, 2) * 128, 128), 128)] = dq_t[...].T
-
         @pl.when((pair == 2) | (pair == 4))
         def _():
             stage_a(done)
@@ -469,8 +471,8 @@
     half16 = lambda *shapes: [pltpu.VMEM(shape, BF16) for shape in shapes]
     full32 = lambda *shapes: [pltpu.VMEM(shape, F32) for shape in shapes]
     scratch = half16(square, (6, 8, 16, WIDTH)) + full32((KEYS, 128)) + half16((KEYS, 128))
-    scratch += half16(square, tall, tall, square, square, wide, wide, square, wide, square, square, square)
-    scratch += half16((128, SLOTS), (2, SLOTS, BLOCK), (2, KEYS, 2 * BLOCK))
+    scratch += half16(square, tall, tall, square, square, square, wide, square, square, square)
+    scratch += half16((2, SLOTS, BLOCK), (2, KEYS, 2 * BLOCK))
     scratch += full32((KEYS, BLOCK), (KEYS, BLOCK), (KEYS, BLOCK)) + half16(tall, tall, tall, tall)
     scratch += half16(*[(KEYS, 128)] * 2, *[(128, SLOTS)] * 4, *[(SLOTS, 128)] * 4, (3, WIDTH, WIDTH))
     scratch += full32((16, 8, 128), (16, 8, 128), (16, 128), (8, 16, 128)) + half16((6, 16, WIDTH))

time: 139 us -> 148 us (1.065)
  Pallas kernels: 138 us -> 147 us
    pallas_call x1, Pallas kernels: 136 us -> 144 us  [whole(): pl.pallas_call(functools.partial(whole_kernel, factor), out_shape=(jax.Sh...]
where the time goes in v7:
time: 148 us; the launch traced here: 147 us
  Pallas kernels  147 us (99%)
    pallas_call x1, Pallas kernels, whole(): pl.pallas_call(functools.partial(whole_kernel, factor), out_shape=(jax.Sh...  144 us

profile of v7, /device:TPU:1, one launch (start us, length us, event | category | flops | bytes accessed | tf_op | source)
XLA Modules:
  0.0 147.4 jit_solution(7396914481007623844)
XLA Ops:
  0.6 144.5 %whole.1 = (bf16[768,768]{1,0:T(8,128)(2,1)}, f32[6,2304]{1,0:T(8,128)}, f32[6,768]{1,0:T(8,128)}) custom-call(bf16[384,1536]{1,0:T(8,128)(2,1)} %feats_ref.1, f32[1536]{0:T(1024)} %gain_ref.1, bf16[1536,768]{1,0:T(8,128)(2,1)} %we_ref.1, s32[1,384]{1,0:T(1,128)} %bitcast.5, bf16[768,768]{1,0:T(8,128)(2,1)} %bitcast.3, bf16[768,2304]{1,0:T(8,128)(2,1)} %wqkv_ref.1, ...), custom_call_target="tpu_custom_call" | custom-call | flops 30000001024 | bytes 16000000 | tf_op jit(solution)/shard_map/whole/pallas_call | solution.py:483
  145.1 2.1 %hand_over.1 = (bf16[768,768]{1,0:T(8,128)(2,1)}, f32[6,2304]{1,0:T(8,128)}, f32[6,768]{1,0:T(8,128)}) custom-call(bf16[768,768]{1,0:T(8,128)(2,1)} %get-tuple-element.9.refs_0_, f32[6,2304]{1,0:T(8,128)} %get-tuple-element.10.refs_1_, f32[6,768]{1,0:T(8,128)} %get-tuple-element.11.refs_2_), custom_call_target="tpu_custom_call" | custom-call | tf_op jit(solution)/shard_map/hand_over/pallas_call | solution.py:519

commit v8 on v5

--- a/solution.py
+++ b/solution.py
@@ -18,8 +18,8 @@
 KEYS = 1536
 BLOCK = 256
 PART = 512
-CHAIN = 64
-PARTS = KEYS // PART
+CHAIN = 128
+PIECES = KEYS // CHAIN
 SIDE = 4
 MASKED = -1e30
 BF16 = jnp.bfloat16
@@ -48,7 +48,7 @@
     feats_ref, gain_ref, we_ref, target_ref, cot_ref, wqkv_ref, wout_ref, place_ref,
     att_ref, oq_ref, oo_ref,
     x, xd, val, bias, q_tok, k_tok, v_tok, do_tok, q_t, k_t, v_t, do_t, x_t, mg, o_t, wout,
-    dq_t, dq_round, dkv, score_0, score_1, grad_p, prob_0, prob_1, grad_0, grad_1,
+    dq_t, dq_round, dkv, score_0, score_1, prob_0, prob_1, grad_0, grad_1,
     key_0, key_1, q_0, q_1, do_0, do_1, qc_0, qc_1, dc_0, dc_1, perm,
     tally, near_all, near, far, own_far,
     g, half, pair_sum, from_a, owned, from_b, spread, from_c,
@@ -360,38 +360,35 @@
             q_rows[a][own, :] = q_t[head_rows(a), :]
             do_rows[a][own, :] = do_t[head_rows(a), :]
 
-        def score_part(step, part):
+        def score_piece(step, piece):
             a, block = step // 3, step % 3
-            rows = slice(part * PART, part * PART + PART)
+            rows = slice(piece * CHAIN, piece * CHAIN + CHAIN)
             s = dot(keys[a][rows, :], q_rows[a][:, block * BLOCK : block * BLOCK + BLOCK])
-            scores[step % 2][rows, :] = s
-            return jnp.max(s, axis=0, keepdims=True)
-
-        def short(part):
-            return [slice(first, first + CHAIN) for first in range(part * PART, part * PART + PART, CHAIN)]
+            peak = jnp.max(s, axis=0, keepdims=True)
+            raw = jnp.exp(s - peak)
+            scores[step % 2][rows, :] = raw
+            return peak, jnp.sum(raw, axis=0, keepdims=True)
+
+        def factors(parts):
+            peak = functools.reduce(jnp.maximum, [p for p, _ in parts])
+            weights = [jnp.exp(p - peak) for p, _ in parts]
+            inverse = 1.0 / sum(w * total for w, (_, total) in zip(weights, parts))
+            return [w * inverse for w in weights]
 
         open_head(0)
-        peaks = [score_part(0, part) for part in range(PARTS)]
+        parts = [score_piece(0, piece) for piece in range(PIECES)]
         open_head(1)
         for step in range(6):
             a, block = step // 3, step % 3
             cols = slice(block * BLOCK, block * BLOCK + BLOCK)
             score = scores[step % 2]
-            peak = functools.reduce(jnp.maximum, peaks)
-            peaks, total = [], jnp.zeros((8, BLOCK), F32)
-            for part in range(PARTS):
+            factor_of = factors(parts)
+            parts = []
+            for piece in range(PIECES):
+                rows = slice(piece * CHAIN, piece * CHAIN + CHAIN)
+                prob[a][rows, cols] = (score[rows, :] * factor_of[piece]).astype(BF16)
                 if step < 5:
-                    peaks.append(score_part(step + 1, part))
-                for rows in short(part):
-                    raw = jnp.exp(score[rows, :] - peak)
-                    score[rows, :] = raw
-                    total = total + jnp.sum(raw.reshape(CHAIN // 8, 8, BLOCK), axis=0)
-            inverse = 1.0 / jnp.sum(total, axis=0, keepdims=True)
-            for part in range(PARTS):
-                whole_part = slice(part * PART, part * PART + PART)
-                grad_p[whole_part, :] = dot(v_tok[whole_part, lanes], do_rows[a][:, cols])
-                for rows in short(part):
-                    prob[a][rows, cols] = (score[rows, :] * inverse).astype(BF16)
+                    parts.append(score_piece(step + 1, piece))
             out = dot(v_t[head_rows(a), :], prob[a][:, cols]).astype(BF16)
             o_t[head_rows(a), cols] = out
             if a == 0:
@@ -399,9 +396,10 @@
             else:
                 close_keys(pair, 0, block)
             delta = jnp.sum(do_t[head_rows(a), cols].astype(F32) * out.astype(F32), axis=0, keepdims=True)
-            for part in range(PARTS):
-                for rows in short(part):
-                    grad[a][rows, cols] = (score[rows, :] * ((grad_p[rows, :] - delta) * inverse)).astype(BF16)
+            for piece in range(PIECES):
+                rows = slice(piece * CHAIN, piece * CHAIN + CHAIN)
+                grad_p = dot(v_tok[rows, lanes], do_rows[a][:, cols])
+                grad[a][rows, cols] = (score[rows, :] * ((grad_p - delta) * factor_of[piece])).astype(BF16)
             dq_t[a * 64 : a * 64 + 64, cols] = (dot(k_t[head_rows(a), :], grad[a][:, cols]) * 0.125).astype(BF16)
             if step == 2:
                 @pl.when((pair == 2) | (pair == 4))
@@ -471,7 +469,7 @@
     scratch = half16(square, (6, 8, 16, WIDTH)) + full32((KEYS, 128)) + half16((KEYS, 128))
     scratch += half16(square, tall, tall, square, square, wide, wide, square, wide, square, square, square)
     scratch += half16((128, SLOTS), (2, SLOTS, BLOCK), (2, KEYS, 2 * BLOCK))
-    scratch += full32((KEYS, BLOCK), (KEYS, BLOCK), (KEYS, BLOCK)) + half16(tall, tall, tall, tall)
+    scratch += full32((KEYS, BLOCK), (KEYS, BLOCK)) + half16(tall, tall, tall, tall)
     scratch += half16(*[(KEYS, 128)] * 2, *[(128, SLOTS)] * 4, *[(SLOTS, 128)] * 4, (3, WIDTH, WIDTH))
     scratch += full32((16, 8, 128), (16, 8, 128), (16, 128), (8, 16, 128)) + half16((6, 16, WIDTH))
     scratch += half16((2, 3, WIDTH, BLOCK), (4, 3, 384, BLOCK), (4, 3, 384, BLOCK), (4, 3, 3, 96, BLOCK))

time: 139 us -> 133 us (0.957)
  Pallas kernels: 138 us -> 131 us
    pallas_call x1, Pallas kernels: 136 us -> 129 us  [whole(): pl.pallas_call(functools.partial(whole_kernel, factor), out_shape=(jax.Sh...]
where the time goes in v8:
time: 133 us; the launch traced here: 132 us
  Pallas kernels  131 us (98%)
    pallas_call x1, Pallas kernels, whole(): pl.pallas_call(functools.partial(whole_kernel, factor), out_shape=(jax.Sh...  129 us

profile of v8, /device:TPU:1, one launch (start us, length us, event | category | flops | bytes accessed | tf_op | source)
XLA Modules:
  0.0 132.1 jit_solution(1057044579914361502)
XLA Ops:
  0.6 129.2 %whole.1 = (bf16[768,768]{1,0:T(8,128)(2,1)}, f32[6,2304]{1,0:T(8,128)}, f32[6,768]{1,0:T(8,128)}) custom-call(bf16[384,1536]{1,0:T(8,128)(2,1)} %feats_ref.1, f32[1536]{0:T(1024)} %gain_ref.1, bf16[1536,768]{1,0:T(8,128)(2,1)} %we_ref.1, s32[1,384]{1,0:T(1,128)} %bitcast.5, bf16[768,768]{1,0:T(8,128)(2,1)} %bitcast.3, bf16[768,2304]{1,0:T(8,128)(2,1)} %wqkv_ref.1, ...), custom_call_target="tpu_custom_call" | custom-call | flops 30000001024 | bytes 16000000 | tf_op jit(solution)/shard_map/whole/pallas_call | solution.py:479
  129.9 2.1 %hand_over.1 = (bf16[768,768]{1,0:T(8,128)(2,1)}, f32[6,2304]{1,0:T(8,128)}, f32[6,768]{1,0:T(8,128)}) custom-call(bf16[768,768]{1,0:T(8,128)(2,1)} %get-tuple-element.9.refs_0_, f32[6,2304]{1,0:T(8,128)} %get-tuple-element.10.refs_1_, f32[6,768]{1,0:T(8,128)} %get-tuple-element.11.refs_2_), custom_call_target="tpu_custom_call" | custom-call | tf_op jit(solution)/shard_map/hand_over/pallas_call | solution.py:515

commit v9 on v8

--- a/solution.py
+++ b/solution.py
@@ -18,7 +18,7 @@
 KEYS = 1536
 BLOCK = 256
 PART = 512
-CHAIN = 128
+CHAIN = 256
 PIECES = KEYS // CHAIN
 SIDE = 4
 MASKED = -1e30

time: 133 us -> 134 us (level)
  Pallas kernels: 131 us -> 133 us
    pallas_call x1, Pallas kernels: 129 us -> 131 us  [whole(): pl.pallas_call(functools.partial(whole_kernel, factor), out_shape=(jax.Sh...]
where the time goes in v9:
time: 134 us
  Pallas kernels  133 us (99%)
    pallas_call x1, Pallas kernels, whole(): pl.pallas_call(functools.partial(whole_kernel, factor), out_shape=(jax.Sh...  131 us

profile of v9, /device:TPU:1, one launch (start us, length us, event | category | flops | bytes accessed | tf_op | source)
XLA Modules:
  0.0 133.8 jit_solution(8616270150989669406)
XLA Ops:
  0.6 130.9 %whole.1 = (bf16[768,768]{1,0:T(8,128)(2,1)}, f32[6,2304]{1,0:T(8,128)}, f32[6,768]{1,0:T(8,128)}) custom-call(bf16[384,1536]{1,0:T(8,128)(2,1)} %feats_ref.1, f32[1536]{0:T(1024)} %gain_ref.1, bf16[1536,768]{1,0:T(8,128)(2,1)} %we_ref.1, s32[1,384]{1,0:T(1,128)} %bitcast.5, bf16[768,768]{1,0:T(8,128)(2,1)} %bitcast.3, bf16[768,2304]{1,0:T(8,128)(2,1)} %wqkv_ref.1, ...), custom_call_target="tpu_custom_call" | custom-call | flops 30000001024 | bytes 16000000 | tf_op jit(solution)/shard_map/whole/pallas_call | solution.py:479
  131.5 2.1 %hand_over.1 = (bf16[768,768]{1,0:T(8,128)(2,1)}, f32[6,2304]{1,0:T(8,128)}, f32[6,768]{1,0:T(8,128)}) custom-call(bf16[768,768]{1,0:T(8,128)(2,1)} %get-tuple-element.9.refs_0_, f32[6,2304]{1,0:T(8,128)} %get-tuple-element.10.refs_1_, f32[6,768]{1,0:T(8,128)} %get-tuple-element.11.refs_2_), custom_call_target="tpu_custom_call" | custom-call | tf_op jit(solution)/shard_map/hand_over/pallas_call | solution.py:515

commit v10 on v8

--- a/solution.py
+++ b/solution.py
@@ -36,7 +36,12 @@
     places = [
         at["core"] * 384 + at[a] * 96 + at[b] * 24 + at[c] * 6 + inner for a, b, c in ORDERS
     ]
-    return np.broadcast_to(np.stack(places)[:, None, :], (3, 8, WIDTH)).astype(np.int32)
+    rank = np.arange(CAP)
+    position = np.where(rank % RATE == 0, rank // RATE, 5 + rank - rank // RATE)
+    group = np.arange(16)[:, None]
+    arrival = np.where(position < 16, group * 16 + position, 256 + group * 32 + position - 16)
+    natural = np.argsort(arrival.reshape(-1))
+    return np.broadcast_to(np.stack(places + [natural])[:, None, :], (4, 8, WIDTH)).astype(np.int32)
 
 
 def dot(a, b):
@@ -47,7 +52,7 @@
     factor,
     feats_ref, gain_ref, we_ref, target_ref, cot_ref, wqkv_ref, wout_ref, place_ref,
     att_ref, oq_ref, oo_ref,
-    x, xd, val, bias, q_tok, k_tok, v_tok, do_tok, q_t, k_t, v_t, do_t, x_t, mg, o_t, wout,
+    x, arrived, xd, val, bias, q_tok, k_tok, v_tok, do_tok, q_t, k_t, v_t, do_t, x_t, mg, o_t, wout,
     dq_t, dq_round, dkv, score_0, score_1, prob_0, prob_1, grad_0, grad_1,
     key_0, key_1, q_0, q_1, do_0, do_1, qc_0, qc_1, dc_0, dc_1, perm,
     tally, near_all, near, far, own_far,
@@ -100,7 +105,10 @@
     ).astype(BF16)
     before_it = dot(one_hot.astype(BF16), earlier)
     rank = jnp.sum(one_hot * before_it, axis=0, keepdims=True)
-    slot = target * CAP + rank.astype(jnp.int32)
+    rank = rank.astype(jnp.int32)
+    eighth = jnp.right_shift(rank, 3)
+    position = jnp.where(rank == eighth * RATE, eighth, 5 + rank - eighth)
+    slot = jnp.where(position < 16, target * 16 + position, 256 + target * 32 + position - 16)
     placing = x_t.at[:, :TILES]
     placing[...] = (lax.broadcasted_iota(jnp.int32, (SLOTS, TILES), 0) == slot).astype(BF16)
     total = jnp.sum(one_hot, axis=1, keepdims=True)
@@ -127,19 +135,26 @@
     ]
     near_all[slide] = tally[slide]
     loads[2].wait()
-    x_copies = []
+    def tile_copies(first_of, height, cols, send, recv):
+        copies = []
+        for k in (7, 8, 6, 9, 5, 10, 4, 11, 3, 12, 2, 13, 1, 14, 0):
+            dev = slides[k]
+            src = placed.at[pl.ds(pl.multiple_of(first_of + dev[0] * height, height), height), cols]
+            dst = arrived.at[pl.ds(pl.multiple_of(first_of + slide * height, height), height), cols]
+            copies.append(begin(src, dst, send.at[k], recv.at[k], dev))
+        return copies
+
+    first_copies = []
     for part in range(2):
         cols = slice(part * 384, part * 384 + 384)
         embedded = dot(normed[:TILES, :], w_e[:WIDTH, cols]) + dot(normed[TILES:, :], w_e[WIDTH:, cols])
         o_t[:TILES, cols] = embedded.astype(BF16)
         placed[:, cols] = dot(placing[...], o_t[:TILES, cols]).astype(BF16)
-        for k in (7, 8, 6, 9, 5, 10, 4, 11, 3, 12, 2, 13, 1, 14, 0):
-            dev = slides[k]
-            src = placed.at[pl.ds(pl.multiple_of(dev[0] * CAP, CAP), CAP), cols]
-            dst = x.at[pl.ds(pl.multiple_of(slide * CAP, CAP), CAP), cols]
-            x_copies.append(begin(src, dst, send_x.at[part, k], recv_x.at[part, k], dev))
-    own = pl.ds(pl.multiple_of(slide * CAP, CAP), CAP)
-    x[own, :] = placed[own, :]
+        first_copies += tile_copies(0, 16, cols, send_x.at[part], recv_x.at[part])
+    rest_copies = tile_copies(256, 32, slice(None), send_x.at[2], recv_x.at[2])
+    for first_of, height in ((0, 16), (256, 32)):
+        own = pl.ds(pl.multiple_of(first_of + slide * height, height), height)
+        arrived[own, :] = placed[own, :]
 
     for copy in near_copies:
         copy.wait_recv()
@@ -171,12 +186,12 @@
         do_tok[:, cols] = d_heads
         do_t[cols, :] = d_heads.T
 
-    row = lax.broadcasted_iota(jnp.int32, (96, SLOTS), 0)
-    pick = lax.broadcasted_iota(jnp.int32, (96, SLOTS), 1) == (row % 16) * CAP + (row // 16) * RATE
+    row = lax.broadcasted_iota(jnp.int32, (96, 256), 0)
+    pick = lax.broadcasted_iota(jnp.int32, (96, 256), 1) == (row % 16) * 16 + row // 16
     pick = pick.astype(BF16)
-    for copy in x_copies:
+    for copy in first_copies:
         copy.wait_recv()
-    rows = dot(pick, x[...]).astype(BF16)
+    rows = dot(pick, arrived[:256, :]).astype(BF16)
     for m in range(6):
         own_far[m] = rows[m * 16 : m * 16 + 16]
 
@@ -187,6 +202,24 @@
     to_down = begin(own_far, xd.at[:, seq], send_z.at[1], recv_z.at[1], down)
     to_side = [begin(own_far, xd.at[:, seq], send_s.at[0], recv_s.at[0], sibling)]
     xd[:, seq] = own_far[...]
+    order = o_t
+    order[...] = (lax.broadcasted_iota(jnp.int32, (SLOTS, SLOTS), 0) == place_ref[3][:1, :]).astype(BF16)
+    for copy in far_copies:
+        copy.wait_recv()
+    for m in range(6):
+        for j in range(8):
+            first = SLOTS + m * 128 + j * 16
+            val[first : first + 16, :] = jnp.where(far[j] > m * RATE, 1.0, 0.0)
+    bias[...] = jnp.where(val[...] > 0.5, 0.0, MASKED).astype(BF16)
+    to_up.wait_recv()
+    relay_up = begin(xd.at[pl.ds(0, 3), down[1]], xd.at[pl.ds(0, 3), down[1]], send_z.at[2], recv_z.at[2], up)
+    to_side.append(begin(xd.at[:, down[1]], xd.at[:, down[1]], send_s.at[1], recv_s.at[1], sibling))
+    to_down.wait_recv()
+    relay_down = begin(xd.at[pl.ds(3, 3), up[1]], xd.at[pl.ds(3, 3), up[1]], send_z.at[3], recv_z.at[3], down)
+    to_side.append(begin(xd.at[:, up[1]], xd.at[:, up[1]], send_s.at[2], recv_s.at[2], sibling))
+    relay_up.wait_recv()
+    relay_down.wait_recv()
+    to_side.append(begin(xd.at[:, across], xd.at[:, across], send_s.at[3], recv_s.at[3], sibling))
 
     def project(first, rows_of):
         @pl.loop(0, 3)
@@ -198,6 +231,18 @@
                 tok[first : first + SLOTS, cols] = part
                 turned[cols, first : first + SLOTS] = part.T
 
+    for copy in to_side:
+        copy.wait_recv()
+    project(SLOTS, lambda cols: xd[:, :, :, cols].reshape(SLOTS, WIDTH if isinstance(cols, slice) else BLOCK))
+
+    for copy in rest_copies:
+        copy.wait_recv()
+
+    @pl.loop(0, 3)
+    def _(c):
+        cols = pl.ds(pl.multiple_of(c * BLOCK, BLOCK), BLOCK)
+        x[:, cols] = dot(order[...], arrived[:, cols]).astype(BF16)
+
     @pl.loop(0, 3)
     def _(c):
         cols = pl.ds(pl.multiple_of(c * BLOCK, BLOCK), BLOCK)
@@ -205,31 +250,9 @@
         q_tok[:, cols] = query
         q_t[cols, :] = query.T
 
-    to_up.wait_recv()
-    relay_up = begin(xd.at[pl.ds(0, 3), down[1]], xd.at[pl.ds(0, 3), down[1]], send_z.at[2], recv_z.at[2], up)
-    to_side.append(begin(xd.at[:, down[1]], xd.at[:, down[1]], send_s.at[1], recv_s.at[1], sibling))
-    to_down.wait_recv()
-    relay_down = begin(xd.at[pl.ds(3, 3), up[1]], xd.at[pl.ds(3, 3), up[1]], send_z.at[3], recv_z.at[3], down)
-    to_side.append(begin(xd.at[:, up[1]], xd.at[:, up[1]], send_s.at[2], recv_s.at[2], sibling))
-
     project(0, lambda cols: x[:, cols])
 
-    relay_up.wait_recv()
-    relay_down.wait_recv()
-    to_side.append(begin(xd.at[:, across], xd.at[:, across], send_s.at[3], recv_s.at[3], sibling))
-    for copy in far_copies:
-        copy.wait_recv()
-    for m in range(6):
-        for j in range(8):
-            first = SLOTS + m * 128 + j * 16
-            val[first : first + 16, :] = jnp.where(far[j] > m * RATE, 1.0, 0.0)
-    bias[...] = jnp.where(val[...] > 0.5, 0.0, MASKED).astype(BF16)
-    for copy in to_side:
-        copy.wait_recv()
-
-    project(SLOTS, lambda cols: xd[:, :, :, cols].reshape(SLOTS, WIDTH if isinstance(cols, slice) else BLOCK))
-
-    for copy in to_side + far_copies + near_copies + x_copies + [to_up, to_down, relay_up, relay_down]:
+    for copy in to_side + far_copies + near_copies + first_copies + rest_copies + [to_up, to_down, relay_up, relay_down]:
         copy.wait_send()
 
     def close_keys(pair, a, third):
@@ -466,7 +489,7 @@
     dma = pltpu.SemaphoreType.DMA
     half16 = lambda *shapes: [pltpu.VMEM(shape, BF16) for shape in shapes]
     full32 = lambda *shapes: [pltpu.VMEM(shape, F32) for shape in shapes]
-    scratch = half16(square, (6, 8, 16, WIDTH)) + full32((KEYS, 128)) + half16((KEYS, 128))
+    scratch = half16(square, square, (6, 8, 16, WIDTH)) + full32((KEYS, 128)) + half16((KEYS, 128))
     scratch += half16(square, tall, tall, square, square, wide, wide, square, wide, square, square, square)
     scratch += half16((128, SLOTS), (2, SLOTS, BLOCK), (2, KEYS, 2 * BLOCK))
     scratch += full32((KEYS, BLOCK), (KEYS, BLOCK)) + half16(tall, tall, tall, tall)
@@ -474,7 +497,7 @@
     scratch += full32((16, 8, 128), (16, 8, 128), (16, 128), (8, 16, 128)) + half16((6, 16, WIDTH))
     scratch += half16((2, 3, WIDTH, BLOCK), (4, 3, 384, BLOCK), (4, 3, 384, BLOCK), (4, 3, 3, 96, BLOCK))
     scratch += full32((4, 3, 96, BLOCK), (4, 3, 3, 24, BLOCK), (4, 3, SIDE, 8, BLOCK), (4, 3, 3, 8, BLOCK))
-    scratch += [dma((8,)), dma((2, 15)), dma((2, 15)), dma((15,)), dma((15,)), dma((7,)), dma((7,))]
+    scratch += [dma((8,)), dma((3, 15)), dma((3, 15)), dma((15,)), dma((15,)), dma((7,)), dma((7,))]
     scratch += [dma((4,))] * 4 + [dma((4, 3))] * 2 + [dma((4, 3, 3))] * 6
     return pl.pallas_call(
         functools.partial(whole_kernel, factor),

time: 133 us -> 136 us (1.023)
  Pallas kernels: 131 us -> 134 us
    pallas_call x1, Pallas kernels: 129 us -> 132 us  [whole(): pl.pallas_call(functools.partial(whole_kernel, factor), out_shape=(jax.Sh...]
where the time goes in v10:
time: 136 us; the launch traced here: 135 us
  Pallas kernels  134 us (99%)
    pallas_call x1, Pallas kernels, whole(): pl.pallas_call(functools.partial(whole_kernel, factor), out_shape=(jax.Sh...  132 us

profile of v10, /device:TPU:1, one launch (start us, length us, event | category | flops | bytes accessed | tf_op | source)
XLA Modules:
  0.0 135.1 jit_solution(17283433474782163337)
XLA Ops:
  0.6 132.1 %whole.1 = (bf16[768,768]{1,0:T(8,128)(2,1)}, f32[6,2304]{1,0:T(8,128)}, f32[6,768]{1,0:T(8,128)}) custom-call(bf16[384,1536]{1,0:T(8,128)(2,1)} %feats_ref.1, f32[1536]{0:T(1024)} %gain_ref.1, bf16[1536,768]{1,0:T(8,128)(2,1)} %we_ref.1, s32[1,384]{1,0:T(1,128)} %bitcast.5, bf16[768,768]{1,0:T(8,128)(2,1)} %bitcast.3, bf16[768,2304]{1,0:T(8,128)(2,1)} %wqkv_ref.1, ...), custom_call_target="tpu_custom_call" | custom-call | flops 30000001024 | bytes 16000000 | tf_op jit(solution)/shard_map/whole/pallas_call | solution.py:502
  132.8 2.1 %hand_over.1 = (bf16[768,768]{1,0:T(8,128)(2,1)}, f32[6,2304]{1,0:T(8,128)}, f32[6,768]{1,0:T(8,128)}) custom-call(bf16[768,768]{1,0:T(8,128)(2,1)} %get-tuple-element.9.refs_0_, f32[6,2304]{1,0:T(8,128)} %get-tuple-element.10.refs_1_, f32[6,768]{1,0:T(8,128)} %get-tuple-element.11.refs_2_), custom_call_target="tpu_custom_call" | custom-call | tf_op jit(solution)/shard_map/hand_over/pallas_call | solution.py:538

commit v11 on v8

--- a/solution.py
+++ b/solution.py
@@ -17,7 +17,6 @@
 SLOTS = 768
 KEYS = 1536
 BLOCK = 256
-PART = 512
 CHAIN = 128
 PIECES = KEYS // CHAIN
 SIDE = 4
@@ -232,14 +231,14 @@
     for copy in to_side + far_copies + near_copies + x_copies + [to_up, to_down, relay_up, relay_down]:
         copy.wait_send()
 
-    def close_keys(pair, a, third):
-        rows = slice(third * PART, third * PART + PART)
-        mine = lax.broadcasted_iota(jnp.int32, (PART, 128), 1) // 64 == a
+    def close_keys(pair, a, which, half_of):
+        rows = slice(half_of * SLOTS, half_of * SLOTS + SLOTS)
+        mine = lax.broadcasted_iota(jnp.int32, (SLOTS, 128), 1) // 64 == a
         slot = lax.rem(pair // 2, 2)
-        for offset, left, right in ((0, grad[a], q_cat[a]), (BLOCK, prob[a], do_cat[a])):
-            lanes = pl.ds(pl.multiple_of(lax.rem(pair, 2) * 128 + offset, 128), 128)
-            part = dot(left[rows, :], right[...]).astype(BF16)
-            dkv[slot, rows, lanes] = jnp.where(mine, part, dkv[slot, rows, lanes])
+        left, right, offset = ((prob[a], do_cat[a], BLOCK), (grad[a], q_cat[a], 0))[which]
+        lanes = pl.ds(pl.multiple_of(lax.rem(pair, 2) * 128 + offset, 128), 128)
+        part = dot(left[rows, :], right[...]).astype(BF16)
+        dkv[slot, rows, lanes] = jnp.where(mine, part, dkv[slot, rows, lanes])
 
     own_half = pl.multiple_of(core * 384, 384)
     its_half = pl.multiple_of((1 - core) * 384, 384)
@@ -281,11 +280,16 @@
     def stage_qkv(r):
         slot = parity(r)
 
+        query_part = dot(x_t[:, :SLOTS], dq_round[slot])
+
         def parts(t):
             if t == 0:
-                return dot(x_t[:, :SLOTS], dq_round[slot])
-            return dot(x_t[...], dkv[slot, :, (t - 1) * BLOCK : t * BLOCK])
-
+                return query_part
+            if t == 1:
+                both.append(dot(x_t[...], dkv[slot]))
+            return both[0][:, (t - 1) * BLOCK : t * BLOCK]
+
+        both = []
         stage_pair(r, parts)
 
     def stage_a(r):
@@ -391,10 +395,8 @@
                     parts.append(score_piece(step + 1, piece))
             out = dot(v_t[head_rows(a), :], prob[a][:, cols]).astype(BF16)
             o_t[head_rows(a), cols] = out
-            if a == 0:
-                close_keys(before, 1, block)
-            else:
-                close_keys(pair, 0, block)
+            for which, half_of in (((0, 0),), ((0, 1), (1, 0)), ((1, 1),))[block]:
+                close_keys(before if a == 0 else pair, 1 - a, which, half_of)
             delta = jnp.sum(do_t[head_rows(a), cols].astype(F32) * out.astype(F32), axis=0, keepdims=True)
             for piece in range(PIECES):
                 rows = slice(piece * CHAIN, piece * CHAIN + CHAIN)
@@ -428,8 +430,9 @@
         def _():
             stage_c(done)
 
-    for third in range(3):
-        close_keys(HEADS // 2 - 1, 1, third)
+    for which in range(2):
+        for half_of in range(2):
+            close_keys(HEADS // 2 - 1, 1, which, half_of)
     for t in range(3):
         pair_copy(0, t).wait_send()
     stage_qkv(2)

time: 133 us -> 128 us (0.962)
  Pallas kernels: 131 us -> 127 us
    pallas_call x1, Pallas kernels: 129 us -> 125 us  [whole(): pl.pallas_call(functools.partial(whole_kernel, factor), out_shape=(jax.Sh...]
where the time goes in v11:
time: 128 us
  Pallas kernels  127 us (99%)
    pallas_call x1, Pallas kernels, whole(): pl.pallas_call(functools.partial(whole_kernel, factor), out_shape=(jax.Sh...  125 us

profile of v11, /device:TPU:1, one launch (start us, length us, event | category | flops | bytes accessed | tf_op | source)
XLA Modules:
  0.0 127.8 jit_solution(4101392902222876206)
XLA Ops:
  0.6 124.9 %whole.1 = (bf16[768,768]{1,0:T(8,128)(2,1)}, f32[6,2304]{1,0:T(8,128)}, f32[6,768]{1,0:T(8,128)}) custom-call(bf16[384,1536]{1,0:T(8,128)(2,1)} %feats_ref.1, f32[1536]{0:T(1024)} %gain_ref.1, bf16[1536,768]{1,0:T(8,128)(2,1)} %we_ref.1, s32[1,384]{1,0:T(1,128)} %bitcast.5, bf16[768,768]{1,0:T(8,128)(2,1)} %bitcast.3, bf16[768,2304]{1,0:T(8,128)(2,1)} %wqkv_ref.1, ...), custom_call_target="tpu_custom_call" | custom-call | flops 30000001024 | bytes 16000000 | tf_op jit(solution)/shard_map/whole/pallas_call | solution.py:482
  125.5 2.1 %hand_over.1 = (bf16[768,768]{1,0:T(8,128)(2,1)}, f32[6,2304]{1,0:T(8,128)}, f32[6,768]{1,0:T(8,128)}) custom-call(bf16[768,768]{1,0:T(8,128)(2,1)} %get-tuple-element.9.refs_0_, f32[6,2304]{1,0:T(8,128)} %get-tuple-element.10.refs_1_, f32[6,768]{1,0:T(8,128)} %get-tuple-element.11.refs_2_), custom_call_target="tpu_custom_call" | custom-call | tf_op jit(solution)/shard_map/hand_over/pallas_call | solution.py:518

commit v12 on v11

--- a/solution.py
+++ b/solution.py
@@ -386,6 +386,7 @@
             a, block = step // 3, step % 3
             cols = slice(block * BLOCK, block * BLOCK + BLOCK)
             score = scores[step % 2]
+            closing = (before if a == 0 else pair, 1 - a)
             factor_of = factors(parts)
             parts = []
             for piece in range(PIECES):
@@ -393,15 +394,17 @@
                 prob[a][rows, cols] = (score[rows, :] * factor_of[piece]).astype(BF16)
                 if step < 5:
                     parts.append(score_piece(step + 1, piece))
+                if piece == PIECES // 2 - 1:
+                    close_keys(*closing, block // 2, block % 2)
             out = dot(v_t[head_rows(a), :], prob[a][:, cols]).astype(BF16)
             o_t[head_rows(a), cols] = out
-            for which, half_of in (((0, 0),), ((0, 1), (1, 0)), ((1, 1),))[block]:
-                close_keys(before if a == 0 else pair, 1 - a, which, half_of)
             delta = jnp.sum(do_t[head_rows(a), cols].astype(F32) * out.astype(F32), axis=0, keepdims=True)
             for piece in range(PIECES):
                 rows = slice(piece * CHAIN, piece * CHAIN + CHAIN)
                 grad_p = dot(v_tok[rows, lanes], do_rows[a][:, cols])
                 grad[a][rows, cols] = (score[rows, :] * ((grad_p - delta) * factor_of[piece])).astype(BF16)
+                if block == 1 and piece == PIECES // 2 - 1:
+                    close_keys(*closing, 1, 1)
             dq_t[a * 64 : a * 64 + 64, cols] = (dot(k_t[head_rows(a), :], grad[a][:, cols]) * 0.125).astype(BF16)
             if step == 2:
                 @pl.when((pair == 2) | (pair == 4))

time: 128 us -> 127 us (level)
  no operation moved by 1% of the time
where the time goes in v12:
time: 127 us
  Pallas kernels  126 us (99%)
    pallas_call x1, Pallas kernels, whole(): pl.pallas_call(functools.partial(whole_kernel, factor), out_shape=(jax.Sh...  124 us

profile of v12, /device:TPU:1, one launch (start us, length us, event | category | flops | bytes accessed | tf_op | source)
XLA Modules:
  0.0 126.9 jit_solution(11286565919863421492)
XLA Ops:
  0.6 124.0 %whole.1 = (bf16[768,768]{1,0:T(8,128)(2,1)}, f32[6,2304]{1,0:T(8,128)}, f32[6,768]{1,0:T(8,128)}) custom-call(bf16[384,1536]{1,0:T(8,128)(2,1)} %feats_ref.1, f32[1536]{0:T(1024)} %gain_ref.1, bf16[1536,768]{1,0:T(8,128)(2,1)} %we_ref.1, s32[1,384]{1,0:T(1,128)} %bitcast.5, bf16[768,768]{1,0:T(8,128)(2,1)} %bitcast.3, bf16[768,2304]{1,0:T(8,128)(2,1)} %wqkv_ref.1, ...), custom_call_target="tpu_custom_call" | custom-call | flops 30000001024 | bytes 16000000 | tf_op jit(solution)/shard_map/whole/pallas_call | solution.py:485
  124.6 2.1 %hand_over.1 = (bf16[768,768]{1,0:T(8,128)(2,1)}, f32[6,2304]{1,0:T(8,128)}, f32[6,768]{1,0:T(8,128)}) custom-call(bf16[768,768]{1,0:T(8,128)(2,1)} %get-tuple-element.9.refs_0_, f32[6,2304]{1,0:T(8,128)} %get-tuple-element.10.refs_1_, f32[6,768]{1,0:T(8,128)} %get-tuple-element.11.refs_2_), custom_call_target="tpu_custom_call" | custom-call | tf_op jit(solution)/shard_map/hand_over/pallas_call | solution.py:521
